TPU v7x, 32 devices: a whole 2x2x4 slice. The times are simulated.
32 devices in a mesh: section: 2 (over x), dp: 16 (over z, y, core).
Axes of the slice: x: 2, y: 2, z: 4, core: 2. Of those that a mesh axis runs over, the one named last changes fastest.
Arguments:
- start_state: bfloat16 [32, 1024, 256], P('dp'), may hold values from -6 to 6
- embedded: bfloat16 [32, 1024, 256], P('dp'), may hold values from -6 to 6
- cotangent: bfloat16 [32, 1024, 256], P('dp'), may hold values from -6 to 6
- segment_ids: int32 [32, 1024], P('dp'), may hold values from 0 to 7, never falling along the last dimension, each value on 1 to 512 neighbouring positions
- pad_lengths: int32 [32], P('dp'), may hold values from 0 to 128
- norm1_gain: float32 [256], replicated, may hold values from 0.1 to 1.9
- norm1_bias: float32 [256], replicated, may hold values from -1.5 to 1.5
- w_qkv: bfloat16 [256, 768], replicated, may hold values from -0.375 to 0.375
- q_bias: float32 [256], replicated, may hold values from -2.5 to 2.5
- v_bias: float32 [256], replicated, may hold values from -2.5 to 2.5
- w_out: bfloat16 [256, 256], replicated, may hold values from -2 to 2
- out_bias: float32 [256], replicated, may hold values from -1.5 to 1.5
- norm2_gain: float32 [256], replicated, may hold values from 0.1 to 1.9
- norm2_bias: float32 [256], replicated, may hold values from -1.5 to 1.5
- w_up: bfloat16 [256, 1024], replicated, may hold values from -0.375 to 0.375
- up_bias: float32 [1024], replicated, may hold values from -2.5 to 2.5
- w_down: bfloat16 [1024, 256], replicated, may hold values from -0.1875 to 0.1875
- down_bias: float32 [256], replicated, may hold values from -1.5 to 1.5
Outputs:
- loop_states: bfloat16 [2, 32, 1024, 256], P('section', 'dp')
- state_grads: float32 [2, 32, 1024, 256], P('section', 'dp')
- embed_grad: float32 [32, 1024, 256], P('dp', 'section')
- grad_norm1_gain: float32 [256], replicated
- grad_norm1_bias: float32 [256], replicated
- grad_w_qkv: float32 [256, 768], replicated
- grad_q_bias: float32 [256], replicated
- grad_v_bias: float32 [256], replicated
- grad_w_out: float32 [256, 256], replicated
- grad_out_bias: float32 [256], replicated
- grad_norm2_gain: float32 [256], replicated
- grad_norm2_bias: float32 [256], replicated
- grad_w_up: float32 [256, 1024], replicated
- grad_up_bias: float32 [1024], replicated
- grad_w_down: float32 [1024, 256], replicated
- grad_down_bias: float32 [256], replicated
All inputs are finite; a program needn't handle non-finite values.
Results may differ from a plain program's by a relative error of at most 0.015.
Values may be sent and summed in bfloat16 or wider, within the bound.
A program may use at most 320 MiB of HBM per device.

v0:
```python
from functools import partial

import jax
import jax.numpy as jnp
from jax import lax
from jax.sharding import PartitionSpec as P

HEADS = 4
HEAD_DIM = 64
MICRO = 2


norm_eps = 1e-05
masked_score = -1e30


def layer_norm(values, norm_gain, norm_shift):
    average = jnp.mean(values, axis=-1, keepdims=True)
    centred = values - average
    spread = jnp.mean(centred * centred, axis=-1, keepdims=True)
    return centred * lax.rsqrt(spread + norm_eps) * norm_gain + norm_shift


def outer_sum(left, right):
    return lax.dot_general(
        left, right, (((0,), (0,)), ((), ())), preferred_element_type=jnp.float32
    )


def against_rows(left, right):
    return lax.dot_general(
        left, right, (((1,), (1,)), ((), ())), preferred_element_type=jnp.float32
    )


def block_mask(segment_ids, pad_lengths, block_start, block_rows):
    length = segment_ids.shape[1]
    key_place = jnp.arange(length, dtype=jnp.int32)
    query_place = block_start + jnp.arange(block_rows, dtype=jnp.int32)
    query_segment = segment_ids[:, block_start : block_start + block_rows]
    same_segment = query_segment[:, :, None] == segment_ids[:, None, :]
    causal = query_place[:, None] >= key_place[None, :]
    key_live = key_place[None, None, :] < (length - pad_lengths)[:, None, None]
    self_pair = query_place[:, None] == key_place[None, :]
    return same_segment & causal[None] & (key_live | self_pair[None])


def split_heads(array):
    row_count, length, model_width = array.shape
    return array.reshape(row_count, length, HEADS, model_width // HEADS)


def split_projected(projected):
    model_width = projected.shape[2] // 3
    queries = split_heads(projected[:, :, :model_width])
    key_rows = split_heads(projected[:, :, model_width : 2 * model_width])
    value_rows = split_heads(projected[:, :, 2 * model_width :])
    return (queries, key_rows, value_rows)


def attention_forward(projected, mask_parts):
    segment_ids, pad_lengths = mask_parts
    row_count, length, triple = projected.shape
    model_width = triple // 3
    queries, key_rows, value_rows = split_projected(projected)
    score_scale = HEAD_DIM ** (-0.5)
    block_rows = min(512, length)
    attended_parts = []
    logsum_parts = []
    for block_start in range(0, length, block_rows):
        allowed_mask = block_mask(segment_ids, pad_lengths, block_start, block_rows)[:, None]
        scores = (
            jnp.einsum(
                "rqhe,rkhe->rhqk",
                queries[:, block_start : block_start + block_rows],
                key_rows,
                preferred_element_type=jnp.float32,
            )
            * score_scale
        )
        scores = jnp.where(allowed_mask, scores, masked_score)
        row_peak = jnp.max(scores, axis=-1, keepdims=True)
        exponents = jnp.exp(scores - row_peak)
        row_total = jnp.sum(exponents, axis=-1, keepdims=True)
        probabilities = (exponents / row_total).astype(jnp.bfloat16)
        attended_parts.append(
            jnp.einsum(
                "rhqk,rkhe->rqhe", probabilities, value_rows, preferred_element_type=jnp.float32
            ).astype(jnp.bfloat16)
        )
        logsum_parts.append((row_peak + jnp.log(row_total))[..., 0])
    attended = jnp.concatenate(attended_parts, axis=1).reshape(row_count, length, model_width)
    logsum = jnp.concatenate(logsum_parts, axis=2)
    return (attended, logsum)


def attention_backward(projected, attended_grad, logsum, mask_parts):
    segment_ids, pad_lengths = mask_parts
    row_count, length, triple = projected.shape
    model_width = triple // 3
    queries, key_rows, value_rows = split_projected(projected)
    grad_heads = split_heads(attended_grad)
    score_scale = HEAD_DIM ** (-0.5)
    block_rows = min(512, length)
    key_grads = jnp.zeros(key_rows.shape, jnp.float32)
    value_grads = jnp.zeros(value_rows.shape, jnp.float32)
    query_parts = []
    for block_start in range(0, length, block_rows):
        allowed_mask = block_mask(segment_ids, pad_lengths, block_start, block_rows)[:, None]
        query_block = queries[:, block_start : block_start + block_rows]
        dslice = grad_heads[:, block_start : block_start + block_rows]
        scores = (
            jnp.einsum("rqhe,rkhe->rhqk", query_block, key_rows, preferred_element_type=jnp.float32)
            * score_scale
        )
        scores = jnp.where(allowed_mask, scores, masked_score)
        probabilities = jnp.exp(scores - logsum[:, :, block_start : block_start + block_rows, None])
        dprobs = jnp.einsum(
            "rqhe,rkhe->rhqk", dslice, value_rows, preferred_element_type=jnp.float32
        )
        row_inner = jnp.sum(probabilities * dprobs, axis=-1, keepdims=True)
        score_grad = (probabilities * (dprobs - row_inner)).astype(jnp.bfloat16)
        query_parts.append(
            jnp.einsum("rhqk,rkhe->rqhe", score_grad, key_rows, preferred_element_type=jnp.float32)
            * score_scale
        )
        key_grads = (
            key_grads
            + jnp.einsum(
                "rhqk,rqhe->rkhe", score_grad, query_block, preferred_element_type=jnp.float32
            )
            * score_scale
        )
        value_grads = value_grads + jnp.einsum(
            "rhqk,rqhe->rkhe",
            probabilities.astype(jnp.bfloat16),
            dslice,
            preferred_element_type=jnp.float32,
        )
    query_grads = jnp.concatenate(query_parts, axis=1)
    joined = jnp.concatenate(
        [
            query_grads.reshape(row_count, length, model_width),
            key_grads.reshape(row_count, length, model_width),
            value_grads.reshape(row_count, length, model_width),
        ],
        axis=-1,
    )
    return joined.astype(jnp.bfloat16)


def forward_layer(inputs, weights, mask_parts):
    (
        norm1_gain,
        norm1_bias,
        w_qkv,
        q_bias,
        v_bias,
        w_out,
        out_bias,
        norm2_gain,
        norm2_bias,
        w_up,
        up_bias,
        w_down,
        down_bias,
    ) = weights
    row_count, length, model_width = inputs.shape
    flat_rows = row_count * length
    normed = (
        layer_norm(inputs, norm1_gain, norm1_bias)
        .astype(jnp.bfloat16)
        .reshape(flat_rows, model_width)
    )
    bias_row = jnp.concatenate([q_bias, jnp.zeros_like(q_bias), v_bias])
    projected = (jnp.dot(normed, w_qkv, preferred_element_type=jnp.float32) + bias_row).astype(
        jnp.bfloat16
    )
    projected = projected.reshape(row_count, length, 3 * model_width)
    attended, logsum = attention_forward(projected, mask_parts)
    branch = (
        jnp.dot(attended.reshape(flat_rows, model_width), w_out, preferred_element_type=jnp.float32)
        + out_bias
    )
    middle = inputs + branch.reshape(row_count, length, model_width)
    normed_two = (
        layer_norm(middle, norm2_gain, norm2_bias)
        .astype(jnp.bfloat16)
        .reshape(flat_rows, model_width)
    )
    hidden = jnp.dot(normed_two, w_up, preferred_element_type=jnp.float32) + up_bias
    active = jax.nn.gelu(hidden, approximate=False).astype(jnp.bfloat16)
    down_part = jnp.dot(active, w_down, preferred_element_type=jnp.float32) + down_bias
    result = middle + down_part.reshape(row_count, length, model_width)
    return (result, (inputs, projected, attended, logsum, middle))


def backward_layer(dresult, saved_parts, weights, mask_parts):
    (
        norm1_gain,
        norm1_bias,
        w_qkv,
        q_bias,
        v_bias,
        w_out,
        out_bias,
        norm2_gain,
        norm2_bias,
        w_up,
        up_bias,
        w_down,
        down_bias,
    ) = weights
    inputs, projected, attended, logsum, middle = saved_parts
    row_count, length, model_width = inputs.shape
    flat_rows = row_count * length
    down_grad = dresult.astype(jnp.bfloat16).reshape(flat_rows, model_width)
    grad_down_bias = jnp.sum(down_grad, axis=0, dtype=jnp.float32)
    normed_two_full, norm_two_pull = jax.vjp(layer_norm, middle, norm2_gain, norm2_bias)
    normed_two = normed_two_full.astype(jnp.bfloat16).reshape(flat_rows, model_width)
    hidden = jnp.dot(normed_two, w_up, preferred_element_type=jnp.float32) + up_bias
    active_full, gelu_pull = jax.vjp(partial(jax.nn.gelu, approximate=False), hidden)
    active = active_full.astype(jnp.bfloat16)
    grad_w_down = outer_sum(active, down_grad)
    active_grad = against_rows(down_grad, w_down)
    hidden_grad = gelu_pull(active_grad)[0].astype(jnp.bfloat16)
    grad_up_bias = jnp.sum(hidden_grad, axis=0, dtype=jnp.float32)
    grad_w_up = outer_sum(normed_two, hidden_grad)
    normed_two_grad = against_rows(hidden_grad, w_up).reshape(row_count, length, model_width)
    middle_part, grad_norm2_gain, grad_norm2_bias = norm_two_pull(normed_two_grad)
    middle_grad = dresult + middle_part
    branch_grad = middle_grad.astype(jnp.bfloat16).reshape(flat_rows, model_width)
    grad_out_bias = jnp.sum(branch_grad, axis=0, dtype=jnp.float32)
    grad_w_out = outer_sum(attended.reshape(flat_rows, model_width), branch_grad)
    attended_grad = (
        against_rows(branch_grad, w_out)
        .astype(jnp.bfloat16)
        .reshape(row_count, length, model_width)
    )
    projected_grad = attention_backward(projected, attended_grad, logsum, mask_parts).reshape(
        flat_rows, 3 * model_width
    )
    column_sums = jnp.sum(projected_grad, axis=0, dtype=jnp.float32)
    grad_q_bias = column_sums[:model_width]
    grad_v_bias = column_sums[2 * model_width :]
    normed_full, norm_one_pull = jax.vjp(layer_norm, inputs, norm1_gain, norm1_bias)
    normed = normed_full.astype(jnp.bfloat16).reshape(flat_rows, model_width)
    grad_w_qkv = outer_sum(normed, projected_grad)
    normed_grad = against_rows(projected_grad, w_qkv).reshape(row_count, length, model_width)
    input_part, grad_norm1_gain, grad_norm1_bias = norm_one_pull(normed_grad)
    input_grad = middle_grad + input_part
    grad_terms = (
        grad_norm1_gain,
        grad_norm1_bias,
        grad_w_qkv,
        grad_q_bias,
        grad_v_bias,
        grad_w_out,
        grad_out_bias,
        grad_norm2_gain,
        grad_norm2_bias,
        grad_w_up,
        grad_up_bias,
        grad_w_down,
        grad_down_bias,
    )
    return (input_grad, grad_terms)


def body(
    start_state,
    embedded,
    cotangent,
    segment_ids,
    pad_lengths,
    norm1_gain,
    norm1_bias,
    w_qkv,
    q_bias,
    v_bias,
    w_out,
    out_bias,
    norm2_gain,
    norm2_bias,
    w_up,
    up_bias,
    w_down,
    down_bias,
):
    weights = (
        norm1_gain,
        norm1_bias,
        w_qkv,
        q_bias,
        v_bias,
        w_out,
        out_bias,
        norm2_gain,
        norm2_bias,
        w_up,
        up_bias,
        w_down,
        down_bias,
    )
    rows_here, length, model_width = start_state.shape
    part_rows = rows_here // MICRO
    totals = tuple((jnp.zeros(leaf_value.shape, jnp.float32) for leaf_value in weights))
    section_at = lax.axis_index("section")
    half_rows = rows_here // 2
    first_row = section_at * half_rows + 0

    def take_rows(array):
        return lax.dynamic_slice_in_dim(array, first_row, part_rows, 0)

    mask_parts = (take_rows(segment_ids), take_rows(pad_lengths))
    embed_part = take_rows(embedded).astype(jnp.float32)
    first_out, first_saved = forward_layer(
        take_rows(start_state).astype(jnp.float32) + embed_part, weights, mask_parts
    )
    first_state = first_out.astype(jnp.bfloat16)
    second_out, second_saved = forward_layer(
        first_state.astype(jnp.float32) + embed_part, weights, mask_parts
    )
    second_grad, second_terms = backward_layer(
        take_rows(cotangent).astype(jnp.float32), second_saved, weights, mask_parts
    )
    first_grad, first_terms = backward_layer(
        second_grad.astype(jnp.bfloat16).astype(jnp.float32), first_saved, weights, mask_parts
    )
    totals = tuple(
        (
            total + term_one + term_two
            for total, term_one, term_two in zip(totals, first_terms, second_terms)
        )
    )
    state_pieces = jnp.stack([first_state, second_out.astype(jnp.bfloat16)])
    grad_pieces = jnp.stack([first_grad, second_grad])
    embed_pieces = first_grad + second_grad
    loop_states = lax.all_to_all(state_pieces, "section", split_axis=0, concat_axis=1, tiled=True)
    state_grads = lax.all_to_all(
        grad_pieces.astype(jnp.bfloat16), "section", split_axis=0, concat_axis=1, tiled=True
    ).astype(jnp.float32)
    embed_grad = lax.all_to_all(
        embed_pieces.astype(jnp.bfloat16), "section", split_axis=1, concat_axis=0, tiled=True
    ).astype(jnp.float32)
    summed = lax.psum(totals, ("section", "dp"))
    return (loop_states, state_grads, embed_grad) + tuple(summed)


def solution(mesh):
    placed = (
        P("dp", None, None),
        P("dp", None, None),
        P("dp", None, None),
        P("dp", None),
        P("dp"),
        P(),
        P(),
        P(),
        P(),
        P(),
        P(),
        P(),
        P(),
        P(),
        P(),
        P(),
        P(),
        P(),
    )
    return jax.shard_map(
        body,
        mesh=mesh,
        in_specs=placed,
        out_specs=(
            P("section", "dp", None, None),
            P("section", "dp", None, None),
            P("dp", "section", None),
            P(),
            P(),
            P(),
            P(),
            P(),
            P(),
            P(),
            P(),
            P(),
            P(),
            P(),
            P(),
            P(),
        ),
        check_vma=False,
    )
```

profile of v0, /device:TPU:0, one launch (start us, length us, event | category | flops | bytes accessed | tf_op | source)
XLA Modules:
  0.0 355.2 jit_solution(8268795523296021381)
XLA Ops:
  14.8 1.8 fusion.37
  16.6 1.8 fusion.148
  18.4 1.9 fusion.1
  21.7 2.1 fusion.84
  23.8 1.8 fusion.149
  25.6 1.9 fusion
  28.9 2.1 fusion.83
  32.3 12.0 %multiply_convert_fusion.5 = (bf16[1024,1024]{1,0:T(8,128)(2,1)S(1)}, f32[1024,1024]{1,0:T(8,128)}, f32[1024,1024]{1,0:T(8,128)}) fusion(f32[1024]{0:T(1024)S(1)} %copy-done.103, bf16[256,1024]{1,0:T(8,128)(2,1)S(1)} %copy-done.94, f32[1,1024,256]{1,2,0:T(8,128)S(1)} %get-tuple-element.107, f32[256]{0:T(256)S(1)} %copy-done.90, f32[256]{0:T(256)S(1)} %copy-done.87, ...), kind=kOutput, calls=%fused_computation.61 | convolution fusion | flops 607387648 | bytes 12072960 | tf_op jit(solution)/shard_map/dot_general | solution.py:191
  46.4 1.8 fusion.151
  48.2 1.8 fusion.152
  50.0 1.9 fusion.3
  51.9 2.1 fusion.86
  54.0 1.9 fusion.2
  55.9 10.8 %fusion.85 = bf16[1,512,4,64]{1,3,2,0:T(8,128)(2,1)S(1)} fusion(bf16[1024,4,64]{0,2,1:T(8,128)(2,1)S(1)} %bitcast.342, f32[4,512,1024]{2,1,0:T(8,128)S(1)} %get-tuple-element.114, f32[4,512]{1,0:T(4,128)S(1)} %fusion.2, f32[4,512]{1,0:T(4,128)S(1)} %get-tuple-element.113), kind=kOutput, calls=%fused_computation.153 | convolution fusion | flops 274857984 | bytes 9191424 | tf_op jit(solution)/shard_map/rhqk,rkhe->rqhe/dot_general | solution.py:87
  68.7 12.1 %multiply_convert_fusion.4 = (bf16[1024,1024]{1,0:T(8,128)(2,1)}, f32[1024,1024]{1,0:T(8,128)S(1)}, f32[1024,1024]{1,0:T(8,128)S(1)}) fusion(f32[1024]{0:T(1024)S(1)} %copy-done.103, bf16[256,1024]{1,0:T(8,128)(2,1)} %param.32, f32[1,1024,256]{1,2,0:T(8,128)S(1)} %get-tuple-element.116, f32[1024]{0:T(1024)S(1)} %fusion.122, ...), kind=kOutput, calls=%fused_computation.48 | convolution fusion | flops 607387648 | bytes 12072960 | tf_op jit(solution)/shard_map/dot_general | solution.py:191
  80.8 2.6 convert_reduce_fusion
  88.8 6.1 %fusion.14 = f32[4,64,1024]{2,1,0:T(8,128)} fusion(f32[4,512,1024]{2,1,0:T(8,128)} %copy-done.4, f32[4,512]{1,0:T(4,128)S(1)} %log_add_fusion.2, bf16[1,1024,4,64]{1,3,2,0:T(8,128)(2,1)S(1)} %bitcast.325), kind=kOutput, calls=%fused_computation.38 | convolution fusion | flops 272629760 | bytes 9707520 | tf_op jit(solution)/shard_map/rhqk,rqhe->rkhe/dot_general | solution.py:134
  94.9 2.6 multiply_reduce_fusion.2
  97.6 4.4 %multiply_reduce_fusion.3 = (f32[4,512]{1,0:T(4,128)S(1)}, f32[4,512,1024]{2,1,0:T(8,128)}) fusion(f32[4,512,1024]{2,1,0:T(8,128)S(1)} %bitcast.306, f32[4,512]{1,0:T(4,128)S(1)} %log_add_fusion.3, bf16[1024,4,64]{0,2,1:T(8,128)(2,1)S(1)} %bitcast.344, bf16[1,1024,4,64]{1,3,2,0:T(8,128)(2,1)S(1)} %bitcast.327), kind=kOutput, calls=%fused_computation.10 | convolution fusion | flops 274724864 | bytes 17580032 | tf_op jit(solution)/shard_map/rqhe,rkhe->rhqk/dot_general | solution.py:118
  101.9 4.3 %multiply_convert_fusion.3 = bf16[4,512,1024]{2,1,0:T(8,128)(2,1)S(1)} fusion(f32[4,512,1024]{2,1,0:T(8,128)} %get-tuple-element.119, f32[4,512,1024]{2,1,0:T(8,128)S(1)} %bitcast.306, f32[4,512]{1,0:T(4,128)S(1)} %get-tuple-element.118, f32[4,512]{1,0:T(4,128)S(1)} %log_add_fusion.3), kind=kLoop, calls=%fused_computation.9 | loop fusion | flops 8388608 | bytes 20987904 | tf_op jit(solution)/shard_map/convert_element_type | solution.py:122
  106.3 2.1 fusion.82
  108.4 1.8 fusion.113
  112.0 2.2 multiply_convert_fusion.2
  123.0 4.0 %convert_reduce_fusion.1 = (f32[1024]{0:T(1024)S(1)}, bf16[1024,1024]{1,0:T(8,128)(2,1)S(1)}) fusion(f32[1024,1024]{1,0:T(8,128)S(1)} %copy-done.111, bf16[1024,256]{1,0:T(8,128)(2,1)S(1)} %copy-done.99, bf16[1,1024,256]{1,2,0:T(8,128)(2,1)S(1)} %get-tuple-element.70, f32[1024,1024]{1,0:T(8,128)} %get-tuple-element.108, f32[1024]{0:T(1024)S(1)} %copy-done.103), kind=kOutput, calls=%fused_computation.41 | convolution fusion | flops 554695680 | bytes 11542528 | tf_op jit(solution)/shard_map/dot_general | solution.py:31
  127.1 2.3 fusion.156
  132.9 6.3 %fusion.10 = f32[4,64,1024]{2,1,0:T(8,128)} fusion(f32[4,512,1024]{2,1,0:T(8,128)} %copy-done.2, f32[4,512]{1,0:T(4,128)S(1)} %copy-done.79, bf16[1,1024,4,64]{1,3,2,0:T(8,128)(2,1)S(1)} %bitcast.329), kind=kOutput, calls=%fused_computation.36 | convolution fusion | flops 272629760 | bytes 9707520 | tf_op jit(solution)/shard_map/rhqk,rqhe->rkhe/dot_general | solution.py:134
  139.2 2.6 multiply_reduce_fusion
  141.9 4.4 %multiply_reduce_fusion.1 = (f32[4,512]{1,0:T(4,128)S(1)}, f32[4,512,1024]{2,1,0:T(8,128)}) fusion(f32[4,512,1024]{2,1,0:T(8,128)S(1)} %bitcast.302, f32[4,512]{1,0:T(4,128)S(1)} %copy-done.80, bf16[1024,4,64]{0,2,1:T(8,128)(2,1)S(1)} %bitcast.340, bf16[1,1024,4,64]{1,3,2,0:T(8,128)(2,1)S(1)} %bitcast.331), kind=kOutput, calls=%fused_computation.4 | convolution fusion | flops 274724864 | bytes 17580032 | tf_op jit(solution)/shard_map/rqhe,rkhe->rhqk/dot_general | solution.py:118
  146.2 4.6 %multiply_convert_fusion.1 = bf16[4,512,1024]{2,1,0:T(8,128)(2,1)S(1)} fusion(f32[4,512,1024]{2,1,0:T(8,128)} %get-tuple-element.123, f32[4,512,1024]{2,1,0:T(8,128)S(1)} %bitcast.302, f32[4,512]{1,0:T(4,128)S(1)} %get-tuple-element.122, f32[4,512]{1,0:T(4,128)S(1)} %copy-done.80), kind=kLoop, calls=%fused_computation.3 | loop fusion | flops 8388608 | bytes 20987904 | tf_op jit(solution)/shard_map/convert_element_type | solution.py:122
  150.8 2.1 fusion.80
  152.9 1.8 fusion.112
  156.5 1.8 multiply_convert_fusion
  163.1 2.7 copy.58
  165.8 1.8 fusion.90
  170.9 3.6 %copy.59 = bf16[1,1024,256]{2,0,1:T(2,128)(2,1)} copy(bf16[1,1024,256]{1,2,0:T(8,128)(2,1)} %get-tuple-element.87) | data formatting | bytes 1048576 | tf_op jit(solution)/shard_map/convert_element_type | solution.py:344
  175.0 4.9 %reduce.52 = bf16[1024,256]{1,0:T(8,128)(2,1)S(1)} reduce(bf16[1024,1,256]{2,1,0:T(2,128)(2,1)} %bitcast.346, bf16[]{:T(256)} %broadcast.733), dimensions={1}, to_apply=%bitcast.211.reduce_sub_computation | reduce | bytes 1048578
  180.7 4.2 %all-to-all-start.2 = ((bf16[2,2,65536]{2,1,0:T(2,128)(2,1)}), bf16[2,2,65536]{2,1,0:T(2,128)(2,1)}, u32[]{:S(2)}, u32[]{:S(2)}) async-start(bf16[2,2,65536]{2,1,0:T(2,128)(2,1)} %reshape.1076), calls=%async_computation.2 | async-start | bytes 1048576 | tf_op jit(solution)/shard_map/all_to_all | solution.py:343
  185.3 2.5 fusion.109
  190.7 1.8 convolution_add_fusion.5
  196.9 2.5 fusion.70
  200.5 4.2 %all-to-all-start = ((bf16[2,1,1024,256]{2,3,1,0:T(8,128)(2,1)}), bf16[2,1,1024,256]{2,3,1,0:T(8,128)(2,1)S(1)}, u32[]{:S(2)}, u32[]{:S(2)}) async-start(bf16[2,1,1024,256]{2,3,1,0:T(8,128)(2,1)} %pad_maximum_fusion.2), calls=%async_computation | async-start | bytes 2097152 | tf_op jit(solution)/shard_map/all_to_all | solution.py:339
  205.8 19.6 %all-to-all-done = bf16[2,1,1024,256]{2,3,1,0:T(8,128)(2,1)S(1)} async-done(((bf16[2,1,1024,256]{2,3,1,0:T(8,128)(2,1)}), bf16[2,1,1024,256]{2,3,1,0:T(8,128)(2,1)S(1)}, u32[]{:S(2)}, u32[]{:S(2)}) %all-to-all-start) | async-done | bytes 1048608 | tf_op jit(solution)/shard_map/all_to_all | solution.py:339
  225.4 3.6 %all-to-all-start.1 = ((bf16[2,1,1024,256]{2,3,1,0:T(8,128)(2,1)}), bf16[2,1,1024,256]{2,3,1,0:T(8,128)(2,1)S(1)}, u32[]{:S(2)}, u32[]{:S(2)}) async-start(bf16[2,1,1024,256]{2,3,1,0:T(8,128)(2,1)} %pad_maximum_fusion.3), calls=%async_computation.1 | async-start | bytes 2097152 | tf_op jit(solution)/shard_map/all_to_all | solution.py:340
  232.2 47.0 %all-reduce = (f32[256]{0:T(256)}, f32[256]{0:T(256)}, f32[256]{0:T(256)}, f32[256]{0:T(256)}, f32[256]{0:T(256)}, /*index=5*/f32[256]{0:T(256)}, f32[256]{0:T(256)}, f32[1024]{0:T(1024)}, f32[256]{0:T(256)}) all-reduce(f32[256]{0:T(256)S(1)} %add.394, f32[256]{0:T(256)S(1)} %add.395, ...), channel_id=1, replica_groups=mesh['section'=2,'dp'=16] {'section','dp'}, use_global_device_ids=true, to_apply=%region_30.31 | all-reduce | flops 3072 | bytes 24576 | tf_op jit(solution)/shard_map/psum | solution.py:346
  283.2 1.8 copy.65
  285.0 56.0 %all-reduce.4.cloned.1.call-done = (f32[256,768]{1,0:T(8,128)}, f32[256,256]{1,0:T(8,128)}, f32[256,1024]{1,0:T(8,128)}, f32[1024,256]{1,0:T(8,128)}) async-done(((f32[256,768]{1,0:T(8,128)}, f32[256,256]{1,0:T(8,128)}, f32[256,1024]{1,0:T(8,128)}, f32[1024,256]{1,0:T(8,128)}), (f32[256,768]{1,0:T(8,128)}, f32[256,256]{1,0:T(8,128)}, f32[256,1024]{1,0:T(8,128)}, ...) | async-done | bytes 3145744 | tf_op jit(solution)/shard_map/psum | solution.py:346
  341.0 2.2 copy.76
  344.8 2.3 copy.78
  (347 shorter events, 64.5 us)
Async XLA Ops:
  7.2 6.6 %copy-start.91 = (f32[256]{0:T(256)S(1)}, f32[256]{0:T(256)}, u32[]{:S(2)}) copy-start(f32[256]{0:T(256)} %param.27) | copy-start | bytes 3076
  7.2 6.6 %copy-start.92 = (f32[256]{0:T(256)S(1)}, f32[256]{0:T(256)}, u32[]{:S(2)}) copy-start(f32[256]{0:T(256)} %param.26) | copy-start | bytes 3076
  7.2 6.6 %copy-start.88 = (f32[256]{0:T(256)S(1)}, f32[256]{0:T(256)}, u32[]{:S(2)}) copy-start(f32[256]{0:T(256)} %param.23) | copy-start | bytes 3076
  7.2 6.6 %copy-start.100 = (bf16[256,768]{1,0:T(8,128)(2,1)S(1)}, bf16[256,768]{1,0:T(8,128)(2,1)}, u32[]{:S(2)}) copy-start(bf16[256,768]{1,0:T(8,128)(2,1)} %param.25) | copy-start | bytes 1179652
  7.2 6.6 %copy-start.104 = (f32[256]{0:T(256)S(1)}, f32[256]{0:T(256)}, u32[]{:S(2)}) copy-start(f32[256]{0:T(256)} %param.24) | copy-start | bytes 3076
  11.0 20.1 %copy-start.8 = (bf16[1,1024,256]{1,2,0:T(8,128)(2,1)}, bf16[1,1024,256]{1,2,0:T(8,128)(2,1)S(1)}, u32[]{:S(2)}) copy-start(bf16[1,1024,256]{1,2,0:T(8,128)(2,1)S(1)} %copy.70) | copy-start | bytes 1572868
  12.5 68.3 %copy-start.67 = (bf16[1,1024,256]{2,1,0:T(8,128)(2,1)}, bf16[1,1024,256]{2,1,0:T(8,128)(2,1)S(1)}, u32[]{:S(2)}) copy-start(bf16[1,1024,256]{2,1,0:T(8,128)(2,1)S(1)} %get-tuple-element.138) | copy-start | bytes 1572868
  14.8 9.0 %copy-start.16 = (bf16[1,1024,256]{1,2,0:T(8,128)(2,1)}, bf16[1,1024,256]{1,2,0:T(8,128)(2,1)S(1)}, u32[]{:S(2)}) copy-start(bf16[1,1024,256]{1,2,0:T(8,128)(2,1)S(1)} %get-tuple-element.93) | copy-start | bytes 1572868
  14.8 9.0 %copy-start.32 = (bf16[1,1024,256]{1,2,0:T(8,128)(2,1)}, bf16[1,1024,256]{1,2,0:T(8,128)(2,1)S(1)}, u32[]{:S(2)}) copy-start(bf16[1,1024,256]{1,2,0:T(8,128)(2,1)S(1)} %get-tuple-element.92) | copy-start | bytes 1572868
  14.8 13.9 %copy-start.47 = (bf16[1,1024,256]{1,2,0:T(8,128)(2,1)}, bf16[1,1024,256]{1,2,0:T(8,128)(2,1)S(1)}, u32[]{:S(2)}) copy-start(bf16[1,1024,256]{1,2,0:T(8,128)(2,1)S(1)} %get-tuple-element.94) | copy-start | bytes 1572868
  31.6 12.7 %copy-start.10 = (f32[1,1024,256]{1,2,0:T(8,128)}, f32[1,1024,256]{1,2,0:T(8,128)S(1)}, u32[]{:S(2)}) copy-start(f32[1,1024,256]{1,2,0:T(8,128)S(1)} %get-tuple-element.107) | copy-start | bytes 3145732
  32.3 12.0 %copy-start.97 = (bf16[1024,256]{1,0:T(8,128)(2,1)S(1)}, bf16[1024,256]{1,0:T(8,128)(2,1)}, u32[]{:S(2)}) copy-start(bf16[1024,256]{1,0:T(8,128)(2,1)} %param.34) | copy-start | bytes 1572868
  32.3 12.0 %copy-start.106 = (f32[256]{0:T(256)S(1)}, f32[256]{0:T(256)}, u32[]{:S(2)}) copy-start(f32[256]{0:T(256)} %param.35) | copy-start | bytes 3076
  45.2 22.6 %copy-start.18 = (bf16[1,1024,256]{1,2,0:T(8,128)(2,1)}, bf16[1,1024,256]{1,2,0:T(8,128)(2,1)S(1)}, u32[]{:S(2)}) copy-start(bf16[1,1024,256]{1,2,0:T(8,128)(2,1)S(1)} %get-tuple-element.110) | copy-start | bytes 1572868
  46.4 9.5 %copy-start.49 = (bf16[1,1024,256]{1,2,0:T(8,128)(2,1)}, bf16[1,1024,256]{1,2,0:T(8,128)(2,1)S(1)}, u32[]{:S(2)}) copy-start(bf16[1,1024,256]{1,2,0:T(8,128)(2,1)S(1)} %get-tuple-element.91) | copy-start | bytes 1572868
  50.0 5.9 %copy-start.5 = (f32[4,512,1024]{2,1,0:T(8,128)}, f32[4,512,1024]{2,1,0:T(8,128)S(1)}, u32[]{:S(2)}) copy-start(f32[4,512,1024]{2,1,0:T(8,128)S(1)} %get-tuple-element.114) | copy-start | bytes 25165828
  68.6 18.5 %copy-start.6 = (f32[1,1024,256]{1,2,0:T(8,128)}, f32[1,1024,256]{1,2,0:T(8,128)S(1)}, u32[]{:S(2)}) copy-start(f32[1,1024,256]{1,2,0:T(8,128)S(1)} %get-tuple-element.116) | copy-start | bytes 3145732
  68.7 12.1 %copy-start.98 = (bf16[1024,256]{1,0:T(8,128)(2,1)S(1)}, bf16[1024,256]{1,0:T(8,128)(2,1)}, u32[]{:S(2)}) copy-start(bf16[1024,256]{1,0:T(8,128)(2,1)} %param.34) | copy-start | bytes 1572868
  87.0 7.9 %slice-start.4 = ((s8[8388608]{0:T(1024)(128)(4,1)}), s8[4194304]{0:T(1024)(128)(4,1)S(1)}, s32[]{:S(2)}) async-start(s8[8388608]{0:T(1024)(128)(4,1)} %bitcast.303), calls=%async_computation.8 | async-start | bytes 8388608
  88.8 8.8 %copy-start.38 = (bf16[1024,256]{0,1:T(8,128)(2,1)}, bf16[1024,256]{0,1:T(8,128)(2,1)S(1)}, u32[]{:S(2)}) copy-start(bf16[1024,256]{0,1:T(8,128)(2,1)S(1)} %convolution_convert_fusion.1) | copy-start | bytes 1572868
  88.8 6.1 %slice-start.5 = ((s8[8388608]{0:T(1024)(128)(4,1)}), s8[4194304]{0:T(1024)(128)(4,1)S(1)}, s32[]{:S(2)}) async-start(s8[8388608]{0:T(1024)(128)(4,1)} %bitcast.303), calls=%async_computation.9 | async-start | bytes 8388608
  88.8 6.1 %copy-start.50 = (bf16[1,1024,256]{1,2,0:T(8,128)(2,1)S(1)}, bf16[1,1024,256]{1,2,0:T(8,128)(2,1)}, u32[]{:S(2)}) copy-start(bf16[1,1024,256]{1,2,0:T(8,128)(2,1)} %copy-done.49) | copy-start | bytes 1572868
  88.8 8.8 %slice-start.6 = ((s8[8388608]{0:T(1024)(128)(4,1)}), s8[4194304]{0:T(1024)(128)(4,1)S(1)}, s32[]{:S(2)}) async-start(s8[8388608]{0:T(1024)(128)(4,1)} %bitcast.305), calls=%async_computation.10 | async-start | bytes 8388608
  111.9 4.7 %copy-start.61 = (bf16[4,64,1024]{2,1,0:T(8,128)(2,1)}, bf16[4,64,1024]{2,1,0:T(8,128)(2,1)S(1)}, u32[]{:S(2)}) copy-start(bf16[4,64,1024]{2,1,0:T(8,128)(2,1)S(1)} %fusion.65) | copy-start | bytes 1572868
  121.8 9.9 %copy-start.21 = (bf16[1,1024,256]{1,2,0:T(8,128)(2,1)}, bf16[1,1024,256]{1,2,0:T(8,128)(2,1)S(1)}, u32[]{:S(2)}) copy-start(bf16[1,1024,256]{1,2,0:T(8,128)(2,1)S(1)} %get-tuple-element.70) | copy-start | bytes 1572868
  131.3 7.9 %slice-start = ((s8[8388608]{0:T(1024)(128)(4,1)}), s8[4194304]{0:T(1024)(128)(4,1)S(1)}, s32[]{:S(2)}) async-start(s8[8388608]{0:T(1024)(128)(4,1)} %bitcast.299), calls=%async_computation.4 | async-start | bytes 8388608
  132.8 9.0 %copy-start.40 = (bf16[1024,256]{0,1:T(8,128)(2,1)}, bf16[1024,256]{0,1:T(8,128)(2,1)S(1)}, u32[]{:S(2)}) copy-start(bf16[1024,256]{0,1:T(8,128)(2,1)S(1)} %convolution_convert_fusion) | copy-start | bytes 1572868
  132.8 6.4 %slice-start.1 = ((s8[8388608]{0:T(1024)(128)(4,1)}), s8[4194304]{0:T(1024)(128)(4,1)S(1)}, s32[]{:S(2)}) async-start(s8[8388608]{0:T(1024)(128)(4,1)} %bitcast.299), calls=%async_computation.5 | async-start | bytes 8388608
  132.8 6.4 %copy-start.48 = (bf16[1,1024,256]{1,2,0:T(8,128)(2,1)S(1)}, bf16[1,1024,256]{1,2,0:T(8,128)(2,1)}, u32[]{:S(2)}) copy-start(bf16[1,1024,256]{1,2,0:T(8,128)(2,1)} %copy-done.47) | copy-start | bytes 1572868
  132.8 9.0 %slice-start.2 = ((s8[8388608]{0:T(1024)(128)(4,1)}), s8[4194304]{0:T(1024)(128)(4,1)S(1)}, s32[]{:S(2)}) async-start(s8[8388608]{0:T(1024)(128)(4,1)} %bitcast.301), calls=%async_computation.6 | async-start | bytes 8388608
  146.2 4.6 %copy-start.17 = (bf16[1,1024,256]{1,2,0:T(8,128)(2,1)S(1)}, bf16[1,1024,256]{1,2,0:T(8,128)(2,1)}, u32[]{:S(2)}) copy-start(bf16[1,1024,256]{1,2,0:T(8,128)(2,1)} %copy-done.16) | copy-start | bytes 1572868
  156.5 4.3 %copy-start.63 = (bf16[4,64,1024]{2,1,0:T(8,128)(2,1)}, bf16[4,64,1024]{2,1,0:T(8,128)(2,1)S(1)}, u32[]{:S(2)}) copy-start(bf16[4,64,1024]{2,1,0:T(8,128)(2,1)S(1)} %fusion.62) | copy-start | bytes 1572868
  160.7 5.1 %copy-start.9 = (bf16[1,1024,256]{1,2,0:T(8,128)(2,1)S(1)}, bf16[1,1024,256]{1,2,0:T(8,128)(2,1)}, u32[]{:S(2)}) copy-start(bf16[1,1024,256]{1,2,0:T(8,128)(2,1)} %copy-done.8) | copy-start | bytes 1572868
  160.7 5.1 %copy-start.82 = (f32[1024]{0:T(1024)S(1)}, f32[1024]{0:T(1024)}, u32[]{:S(2)}) copy-start(f32[1024]{0:T(1024)} %copy-done.81) | copy-start | bytes 12292
  160.7 5.1 %copy-start.84 = (f32[1024]{0:T(1024)S(1)}, f32[1024]{0:T(1024)}, u32[]{:S(2)}) copy-start(f32[1024]{0:T(1024)} %copy-done.83) | copy-start | bytes 12292
  161.5 6.1 %copy-start.86 = (f32[1024]{0:T(1024)S(1)}, f32[1024]{0:T(1024)}, u32[]{:S(2)}) copy-start(f32[1024]{0:T(1024)} %copy-done.85) | copy-start | bytes 12292
  163.1 6.1 %copy-start.15 = (f32[1,1024,256]{1,2,0:T(8,128)S(1)}, f32[1,1024,256]{1,2,0:T(8,128)}, u32[]{:S(2)}) copy-start(f32[1,1024,256]{1,2,0:T(8,128)} %copy-done.13) | copy-start | bytes 3145732
  163.1 6.1 %copy-start.22 = (bf16[1,1024,256]{1,2,0:T(8,128)(2,1)S(1)}, bf16[1,1024,256]{1,2,0:T(8,128)(2,1)}, u32[]{:S(2)}) copy-start(bf16[1,1024,256]{1,2,0:T(8,128)(2,1)} %copy-done.21) | copy-start | bytes 1572868
  163.1 6.1 %copy-start.31 = (bf16[1,1024,256]{1,2,0:T(8,128)(2,1)S(1)}, bf16[1,1024,256]{1,2,0:T(8,128)(2,1)}, u32[]{:S(2)}) copy-start(bf16[1,1024,256]{1,2,0:T(8,128)(2,1)} %copy.69) | copy-start | bytes 1572868
  175.0 12.8 %copy-start.12 = (f32[1,1024,256]{1,2,0:T(8,128)S(1)}, f32[1,1024,256]{1,2,0:T(8,128)}, u32[]{:S(2)}) copy-start(f32[1,1024,256]{1,2,0:T(8,128)} %copy-done.10) | copy-start | bytes 3145732
  180.7 19.8 %all-to-all-start.2 = ((bf16[2,2,65536]{2,1,0:T(2,128)(2,1)}), bf16[2,2,65536]{2,1,0:T(2,128)(2,1)}, u32[]{:S(2)}, u32[]{:S(2)}) async-start(bf16[2,2,65536]{2,1,0:T(2,128)(2,1)} %reshape.1076), calls=%async_computation.2 | async-start | bytes 1048576 | tf_op jit(solution)/shard_map/all_to_all | solution.py:343
  185.0 156.0 %all-reduce.4.cloned.1.call-start = ((), (), s32[]{:S(2)}) async-start(), calls=%async_computation.3 | async-start | bytes 6291456 | tf_op jit(solution)/shard_map/psum | solution.py:346
  196.9 7.8 %copy-start.75 = (bf16[1,1,1024,256]{2,3,1,0:T(8,128)(2,1)S(1)}, bf16[1,1,1024,256]{2,3,1,0:T(8,128)(2,1)}, u32[]{:S(2)}) copy-start(bf16[1,1,1024,256]{2,3,1,0:T(8,128)(2,1)} %get-tuple-element.88) | copy-start | bytes 1572868
  199.4 29.6 %copy-start.93 = (f32[256]{0:T(256)S(1)}, f32[256]{0:T(256)}, u32[]{:S(2)}) copy-start(f32[256]{0:T(256)} %get-tuple-element.130) | copy-start | bytes 3076
  200.5 24.9 %all-to-all-start = ((bf16[2,1,1024,256]{2,3,1,0:T(8,128)(2,1)}), bf16[2,1,1024,256]{2,3,1,0:T(8,128)(2,1)S(1)}, u32[]{:S(2)}, u32[]{:S(2)}) async-start(bf16[2,1,1024,256]{2,3,1,0:T(8,128)(2,1)} %pad_maximum_fusion.2), calls=%async_computation | async-start | bytes 2097152 | tf_op jit(solution)/shard_map/all_to_all | solution.py:339
  225.4 57.6 %all-to-all-start.1 = ((bf16[2,1,1024,256]{2,3,1,0:T(8,128)(2,1)}), bf16[2,1,1024,256]{2,3,1,0:T(8,128)(2,1)S(1)}, u32[]{:S(2)}, u32[]{:S(2)}) async-start(bf16[2,1,1024,256]{2,3,1,0:T(8,128)(2,1)} %pad_maximum_fusion.3), calls=%async_computation.1 | async-start | bytes 2097152 | tf_op jit(solution)/shard_map/all_to_all | solution.py:340
  283.2 64.9 %copy-start.1 = (bf16[2,1024,256]{2,1,0:T(8,128)(2,1)S(1)}, bf16[2,1024,256]{2,1,0:T(8,128)(2,1)}, u32[]{:S(2)}) copy-start(bf16[2,1024,256]{2,1,0:T(8,128)(2,1)} %param.18) | copy-start | bytes 3145732
  341.0 6.1 %copy-start.76 = (f32[1024,256]{1,0:T(8,128)S(1)}, f32[1024,256]{1,0:T(8,128)}, u32[]{:S(2)}) copy-start(f32[1024,256]{1,0:T(8,128)} %get-tuple-element.154) | copy-start | bytes 3145732
  (76 other events, 152.3 us)
Sparse Core Ops, SparseCore 0:
  197.0 143.9 all-reduce.3
where the time goes:
time: 360 us; the launch traced here: 355 us
  matrix products  121 us (34%)
  waiting for transfers between devices  75.6 us (21%)
  blocking collectives  47 us (13%)
  other arithmetic  43.9 us (12%)
  local copies, waits for them, and re-layouts  38.5 us (11%)
  between operations  16.7 us (5%)
  starting transfers between devices  12.3 us (3%)
    psum x1, waiting for transfers between devices, body(): summed = lax.psum(totals, ('section', 'dp'))  56 us
    psum x1, blocking collectives, body(): summed = lax.psum(totals, ('section', 'dp'))  47 us
    dot_general x2, matrix products, forward_layer(): jnp.dot(normed_two, w_up, preferred_element_type=jnp.float32) + up_bias  24.1 us
    unnamed x253, local copies, waits for them, and re-layouts  22.9 us
    all_to_all x1, waiting for transfers between devices, body(): lax.all_to_all(state_pieces, 'section', split_axis=0, concat_axis=1, tile...  19.6 us
    dot_general x4, matrix products, attention_forward(): jnp.einsum('rhqk,rkhe->rqhe', probabilities, value_rows, preferred_elemen...  17.1 us
    dot_general x4, matrix products, attention_backward(): jnp.einsum('rhqk,rqhe->rkhe', probabilities.astype(jnp.bfloat16), dslice,...  15.9 us
    dot_general x8, matrix products, against_rows(): lax.dot_general(left, right, (((1,), (1,)), ((), ())), preferred_element_...  14.5 us
  transfers between devices with their start and end apart: 4, of which 2 were waited for; matrix products, arithmetic and copies ran while one was open for 7% of the time, Pallas kernels for 0%

commit v1 on v0

v1 whole, which is shorter than its diff:
```python
from functools import partial

import jax
import jax.numpy as jnp
from jax import lax
from jax.experimental import pallas as pl
from jax.experimental.pallas import tpu as pltpu
from jax.sharding import PartitionSpec as P

HEADS = 4
HEAD_DIM = 64
BLOCK = 256
SPAN = 512
norm_eps = 1e-05
masked_score = -1e30
bf16 = jnp.bfloat16
f32 = jnp.float32


def mul(left, right):
    return jnp.dot(left, right, preferred_element_type=f32)


def mul_rows(left, right):
    return lax.dot_general(left, right, (((1,), (1,)), ((), ())), preferred_element_type=f32)


def mul_columns(left, right):
    return lax.dot_general(left, right, (((0,), (0,)), ((), ())), preferred_element_type=f32)


def row_of(ref):
    return ref[...].reshape(1, ref.shape[0])


def eight_sums(values):
    rows, width = values.shape
    return jnp.sum(values.reshape(rows // 8, 8, width), axis=0)


def normalise(x):
    average = jnp.mean(x, axis=-1, keepdims=True)
    centred = x - average
    spread = jnp.mean(centred * centred, axis=-1, keepdims=True)
    scale = lax.rsqrt(spread + norm_eps)
    return centred * scale, scale


def norm_back(cotangent, gain, hat, scale):
    scaled = cotangent * gain
    first = jnp.mean(scaled, axis=-1, keepdims=True)
    second = jnp.mean(scaled * hat, axis=-1, keepdims=True)
    return scale * (scaled - first - hat * second)


def blocks_of(length):
    result, store = [], 0
    for b in range(length // BLOCK):
        first = max(0, b - SPAN // BLOCK)
        result.append((b, first, store))
        store += (b + 1 - first) * BLOCK
    return result, store


N1G, N1B, QB, VB, OB, N2G, N2B, DB, UB = (256 * i for i in range(9))
SUMS = 256 * 12


def compute_kernel(
    start_hbm, emb_hbm, cot_hbm, seg_ref, pad_ref,
    g1_ref, b1_ref, wqkv_ref, qb_ref, vb_ref, wout_ref, ob_ref, g2_ref, b2_ref, wup_ref, ub_ref,
    wdown_ref, db_ref,
    state_ref, grad_ref, gqkv_ref, gout_ref, gup_ref, gdown_ref, sums_ref,
    start_v, emb_v, cot_v, qx, kx, xbuf, hat1, scale1, normed1, qa, qt, ka, va, expo, inverse,
    outcome, hat2, scale2, normed2, active, slope, hgrad, branch, mgrad, dout, goa, gt,
    dq, dkt, dvt, pgrad, gdown_t, in_sem,
):
    length, width = xbuf.shape
    count = length // BLOCK
    part = lax.axis_index("section")
    loads = [
        pltpu.make_async_copy(hbm.at[part], dest, in_sem.at[i])
        for i, (hbm, dest) in enumerate(((start_hbm, start_v), (emb_hbm, emb_v), (cot_hbm, cot_v)))
    ]
    for load in loads:
        load.start()

    lane = lax.broadcasted_iota(jnp.int32, (128, 128), 1) & 63
    for c in range(length // 128):
        tokens = slice(c * 128, c * 128 + 128)
        ids = jnp.where(part == 0, seg_ref[0:1, tokens], seg_ref[1:2, tokens]).astype(f32)
        ids = jnp.broadcast_to(ids, (128, 128)).T.astype(jnp.int32)
        same = ids == lane
        qx[tokens, :] = jnp.where((lane < 8) & jnp.logical_not(same), masked_score, 0.0).astype(bf16)
        kx[tokens, :] = jnp.where(same, 1.0, 0.0).astype(bf16)

    for load in loads:
        load.wait()
    xbuf[...] = start_v[...].astype(f32) + emb_v[...].astype(f32)

    low_half = lax.broadcasted_iota(jnp.int32, (BLOCK, 128), 1) < 64
    row_at = lax.broadcasted_iota(jnp.int32, (BLOCK, BLOCK), 0)
    col_at = lax.broadcasted_iota(jnp.int32, (BLOCK, BLOCK), 1)
    ones = jnp.ones((BLOCK, 128), bf16)

    def rows_at(b):
        return pl.ds(pl.multiple_of(b * BLOCK, BLOCK), BLOCK)

    def forward(t, _):
        def project(b, _):
            rows = rows_at(b)
            hat, scale = normalise(xbuf[rows, :])
            normed = (hat * row_of(g1_ref) + row_of(b1_ref)).astype(bf16)
            hat1[t, rows, :] = hat
            scale1[t, rows, :] = jnp.broadcast_to(scale, (BLOCK, 128))
            normed1[t, rows, :] = normed
            q = (mul(normed, wqkv_ref[:, :width]) + row_of(qb_ref)).astype(bf16)
            q = q * jnp.asarray(HEAD_DIM**-0.5, bf16)
            k = mul(normed, wqkv_ref[:, width : 2 * width]).astype(bf16)
            v = (mul(normed, wqkv_ref[:, 2 * width :]) + row_of(vb_ref)).astype(bf16)
            qt[t, :, rows] = q.T
            for pair in range(HEADS // 2):
                lanes = slice(pair * 128, pair * 128 + 128)
                for h, mine in ((2 * pair, low_half), (2 * pair + 1, jnp.logical_not(low_half))):
                    qa[h, rows, :] = jnp.where(mine, q[:, lanes], qx[rows, :])
                    ka[t, h, rows, :] = jnp.where(mine, k[:, lanes], kx[rows, :])
                    va[t, h, rows, :] = jnp.where(mine, v[:, lanes], ones)
            return 0

        lax.fori_loop(0, count, project, 0)

        def attend(pair, _):
            for b, first, store in blocks_of(length)[0]:
                rows = slice(b * BLOCK, b * BLOCK + BLOCK)
                keys = slice(first * BLOCK, b * BLOCK + BLOCK)
                wide = (b + 1 - first) * BLOCK
                live = col_at + b * BLOCK < length - pad_ref[part]
                diagonal = (row_at == col_at) | ((row_at > col_at) & live)
                results = []
                for parity in range(2):
                    h = 2 * pair + parity
                    scores = mul_rows(qa[h, rows, :], ka[t, h, keys, :])
                    last = jnp.where(diagonal, scores[:, wide - BLOCK :], masked_score)
                    if wide > BLOCK:
                        scores = jnp.concatenate([scores[:, : wide - BLOCK], last], axis=1)
                    else:
                        scores = last
                    peak = jnp.max(scores, axis=1, keepdims=True)
                    exps = jnp.exp(scores - peak).astype(bf16)
                    expo[t, h, :, store : store + wide] = exps
                    results.append(mul(exps, va[t, h, keys, :]))
                top = jnp.where(low_half, results[0], results[1])
                total = pltpu.roll(jnp.where(low_half, results[1], results[0]), 64, 1)
                inv = 1.0 / total
                inverse[t, pair, rows, :] = inv
                outcome[t, pair, rows, :] = top * inv
            return 0

        lax.fori_loop(0, HEADS // 2, attend, 0)

        def feed(b, _):
            rows = rows_at(b)
            middle = xbuf[rows, :] + row_of(ob_ref)
            for pair in range(HEADS // 2):
                middle = middle + mul(outcome[t, pair, rows, :].astype(bf16), wout_ref[pair * 128 : pair * 128 + 128, :])
            hat, scale = normalise(middle)
            normed = (hat * row_of(g2_ref) + row_of(b2_ref)).astype(bf16)
            hat2[t, rows, :] = hat
            scale2[t, rows, :] = jnp.broadcast_to(scale, (BLOCK, 128))
            normed2[t, rows, :] = normed
            total = middle + row_of(db_ref)
            for c in range(wup_ref.shape[1] // 256):
                columns = slice(c * 256, c * 256 + 256)
                hidden = mul(normed, wup_ref[:, columns]) + row_of(ub_ref)[:, columns]
                phi = 0.5 + 0.5 * lax.erf(hidden * 0.7071067811865476)
                density = 0.3989422804014327 * jnp.exp(-0.5 * hidden * hidden)
                act = (hidden * phi).astype(bf16)
                active[t, rows, columns] = act
                slope[t, rows, columns] = (phi + hidden * density).astype(bf16)
                total = total + mul(act, wdown_ref[columns, :])
            state = total.astype(bf16)
            state_ref[t, 0, rows, :] = state
            xbuf[rows, :] = state.astype(f32) + emb_v[rows, :].astype(f32)
            return 0

        lax.fori_loop(0, count, feed, 0)
        return 0

    lax.fori_loop(0, 2, forward, 0)

    sums_ref[...] = jnp.zeros_like(sums_ref)
    gqkv_ref[...] = jnp.zeros_like(gqkv_ref)
    gout_ref[...] = jnp.zeros_like(gout_ref)
    gup_ref[...] = jnp.zeros_like(gup_ref)
    gdown_t[...] = jnp.zeros_like(gdown_t)
    dout[...] = cot_v[...]

    def add_sums(at, values):
        columns = slice(at, at + values.shape[1])
        sums_ref[:, columns] += eight_sums(values)

    def backward(step, _):
        t = 1 - step

        def feed_back(b, _):
            rows = rows_at(b)
            down = dout[rows, :]
            down_wide = down.astype(f32)
            add_sums(DB, down_wide)
            cotangent = jnp.zeros((BLOCK, width), f32)
            for c in range(wup_ref.shape[1] // 256):
                columns = slice(c * 256, c * 256 + 256)
                up = mul_rows(down, wdown_ref[columns, :]) * slope[t, rows, columns].astype(f32)
                up = up.astype(bf16)
                hgrad[rows, columns] = up
                add_sums(UB + c * 256, up.astype(f32))
                cotangent = cotangent + mul_rows(up, wup_ref[:, columns])
            hat = hat2[t, rows, :]
            add_sums(N2G, cotangent * hat)
            add_sums(N2B, cotangent)
            middle = down_wide + norm_back(cotangent, row_of(g2_ref), hat, scale2[t, rows, 0:1])
            mgrad[rows, :] = middle
            low = middle.astype(bf16)
            branch[rows, :] = low
            add_sums(OB, low.astype(f32))
            attended_grad = mul_rows(low, wout_ref[...]).astype(bf16)
            for pair in range(HEADS // 2):
                grad = attended_grad[:, pair * 128 : pair * 128 + 128].astype(f32)
                scaled = (grad * inverse[t, pair, rows, :]).astype(bf16)
                product = scaled.astype(f32) * outcome[t, pair, rows, :]
                gt[pair * 128 : pair * 128 + 128, rows] = scaled.T
                lane_of = lax.broadcasted_iota(jnp.int32, (BLOCK, 128), 1)
                for parity in range(2):
                    mine = low_half if parity == 0 else jnp.logical_not(low_half)
                    inner = -jnp.sum(jnp.where(mine, product, 0.0), axis=1, keepdims=True)
                    high = inner.astype(bf16).astype(f32)
                    rest = inner - high
                    spot = lane_of - (64 - parity * 64)
                    extra = jnp.where(spot == 0, high, jnp.where(spot == 1, rest, 0.0))
                    goa[2 * pair + parity, rows, :] = jnp.where(mine, scaled, extra.astype(bf16))
            return 0

        lax.fori_loop(0, count, feed_back, 0)

        gdown_t[...] += mul_columns(dout[...], active[t])
        gup_ref[...] += mul_columns(normed2[t], hgrad[...])
        for pair in range(HEADS // 2):
            gout_ref[pair * 128 : pair * 128 + 128, :] += mul_columns(
                outcome[t, pair].astype(bf16), branch[...]
            )

        for b, first, store in reversed(blocks_of(length)[0]):
            rows = slice(b * BLOCK, b * BLOCK + BLOCK)
            keys = slice(first * BLOCK, b * BLOCK + BLOCK)
            wide = (b + 1 - first) * BLOCK

            def attend_back(pair, _):
                parts = []
                for parity in range(2):
                    h = 2 * pair + parity
                    head_rows = pl.ds(pl.multiple_of(h * HEAD_DIM, HEAD_DIM), HEAD_DIM)
                    exps = expo[t, h, :, store : store + wide]
                    slopes = mul_rows(goa[h, rows, :], va[t, h, keys, :])
                    score_grad = (exps.astype(f32) * slopes).astype(bf16)
                    parts.append(mul(score_grad, ka[t, h, keys, :]))
                    key_part = mul(qt[t, head_rows, rows], score_grad)
                    value_part = mul(gt[head_rows, rows], exps)
                    for kb in range(first, b + 1):
                        mine = slice((kb - first) * BLOCK, (kb - first) * BLOCK + BLOCK)
                        there = slice(kb * BLOCK, kb * BLOCK + BLOCK)
                        if b == min(count - 1, kb + SPAN // BLOCK):
                            dkt[head_rows, there] = key_part[:, mine]
                            dvt[head_rows, there] = value_part[:, mine]
                        else:
                            dkt[head_rows, there] += key_part[:, mine]
                            dvt[head_rows, there] += value_part[:, mine]
                dq[pair] = jnp.where(low_half, parts[0], parts[1])
                return 0

            lax.fori_loop(0, HEADS // 2, attend_back, 0)
            for pair in range(HEADS // 2):
                pgrad[rows, pair * 128 : pair * 128 + 128] = (dq[pair] * HEAD_DIM**-0.5).astype(bf16)
            pgrad[rows, width : 2 * width] = dkt[:, rows].T.astype(bf16)
            pgrad[rows, 2 * width :] = dvt[:, rows].T.astype(bf16)
            part_grad = pgrad[rows, :]
            add_sums(QB, part_grad[:, :width].astype(f32))
            add_sums(VB, part_grad[:, 2 * width :].astype(f32))
            cotangent = mul_rows(part_grad, wqkv_ref[...])
            hat = hat1[t, rows, :]
            add_sums(N1G, cotangent * hat)
            add_sums(N1B, cotangent)
            x_grad = mgrad[rows, :] + norm_back(cotangent, row_of(g1_ref), hat, scale1[t, rows, 0:1])
            grad_ref[t, 0, rows, :] = x_grad
            dout[rows, :] = x_grad.astype(bf16)

        gqkv_ref[...] += mul_columns(normed1[t], pgrad[...])
        return 0

    lax.fori_loop(0, 2, backward, 0)
    gdown_ref[...] = gdown_t[...].T


def local_part(args):
    start = args[0]
    _, length, width = start.shape
    hidden = args[15].shape[0]
    vmem = pl.BlockSpec(memory_space=pltpu.VMEM)
    smem = pl.BlockSpec(memory_space=pltpu.SMEM)
    hbm = pl.BlockSpec(memory_space=pl.ANY)
    count = length // BLOCK
    pairs = HEADS // 2

    def V(*shape, dtype=bf16):
        return pltpu.VMEM(shape, dtype)

    return pl.pallas_call(
        compute_kernel,
        name="block_both_ways",
        in_specs=[hbm, hbm, hbm, vmem, smem] + [vmem] * 13,
        out_specs=[vmem] * 7,
        out_shape=[
            jax.ShapeDtypeStruct((2, 1, length, width), bf16),
            jax.ShapeDtypeStruct((2, 1, length, width), f32),
            jax.ShapeDtypeStruct((width, 3 * width), f32),
            jax.ShapeDtypeStruct((width, width), f32),
            jax.ShapeDtypeStruct((width, hidden), f32),
            jax.ShapeDtypeStruct((hidden, width), f32),
            jax.ShapeDtypeStruct((8, SUMS), f32),
        ],
        scratch_shapes=[
            V(length, width),
            V(length, width),
            V(length, width),
            V(length, 128),
            V(length, 128),
            V(length, width, dtype=f32),
            V(2, length, width, dtype=f32),
            V(2, length, 128, dtype=f32),
            V(2, length, width),
            V(HEADS, length, 128),
            V(2, width, length),
            V(2, HEADS, length, 128),
            V(2, HEADS, length, 128),
            V(2, HEADS, BLOCK, blocks_of(length)[1]),
            V(2, pairs, length, 128, dtype=f32),
            V(2, pairs, length, 128, dtype=f32),
            V(2, length, width, dtype=f32),
            V(2, length, 128, dtype=f32),
            V(2, length, width),
            V(2, length, hidden),
            V(2, length, hidden),
            V(length, hidden),
            V(length, width),
            V(length, width, dtype=f32),
            V(length, width),
            V(HEADS, length, 128),
            V(width, length),
            V(pairs, BLOCK, 128, dtype=f32),
            V(width, length, dtype=f32),
            V(width, length, dtype=f32),
            V(length, 3 * width),
            V(width, hidden, dtype=f32),
            pltpu.SemaphoreType.DMA((3,)),
        ],
        compiler_params=pltpu.CompilerParams(vmem_limit_bytes=60 << 20),
    )(*args)


def body(*args):
    states, grads, gqkv, gout, gup, gdown, sums = local_part(args)
    sums = jnp.sum(sums, axis=0)

    def piece(at, size=256):
        return sums[at : at + size]

    totals = (
        piece(N1G), piece(N1B), gqkv, piece(QB), piece(VB), gout, piece(OB), piece(N2G), piece(N2B),
        gup, piece(UB, 1024), gdown, piece(DB),
    )
    embed = grads[0] + grads[1]
    loop_states = lax.all_to_all(states, "section", split_axis=0, concat_axis=1, tiled=True)
    state_grads = lax.all_to_all(
        grads.astype(bf16), "section", split_axis=0, concat_axis=1, tiled=True
    ).astype(f32)
    embed_grad = lax.all_to_all(
        embed.astype(bf16), "section", split_axis=1, concat_axis=0, tiled=True
    ).astype(f32)
    summed = lax.psum(totals, ("section", "dp"))
    return (loop_states, state_grads, embed_grad) + tuple(summed)


def solution(mesh):
    rows = P("dp", None, None)
    return jax.shard_map(
        body,
        mesh=mesh,
        in_specs=(rows, rows, rows, P("dp", None), P("dp")) + (P(),) * 13,
        out_specs=(
            P("section", "dp", None, None),
            P("section", "dp", None, None),
            P("dp", "section", None),
        )
        + (P(),) * 13,
        check_vma=False,
    )
```

time: 360 us -> 239 us (0.66); the launches traced: 355 us -> 238 us
  matrix products: 121 us -> 0 us
  Pallas kernels: 0 us -> 57.5 us
  other arithmetic: 43.9 us -> 8.05 us
  local copies, waits for them, and re-layouts: 38.5 us -> 10.5 us
  waiting for transfers between devices: 75.6 us -> 91 us
    dot_general x48 -> x0, matrix products: 121 us -> none  [the longest x2 24.1 us: forward_layer(): jnp.dot(normed_two, w_up, preferred_element_type=jnp.float32) + up_bias]
    pallas_call x0 -> x1, Pallas kernels: none -> 57.5 us  [local_part(): pl.pallas_call(compute_kernel, name='block_both_ways', in_specs=[hbm, hbm...]
    reduce_sum x22 -> x1, other arithmetic: 17.7 us -> 0.03 us  [body(): sums = jnp.sum(sums, axis=0)]
    unnamed x253 -> x23, local copies, waits for them, and re-layouts: 22.9 us -> 9.7 us
    convert_element_type x6 -> x3, other arithmetic: 14.7 us -> 4.2 us  [the longest x1 1.65 us: body(): embed.astype(bf16)]
    psum x1, waiting for transfers between devices: 56 us -> 63.9 us  [body(): summed = lax.psum(totals, ('section', 'dp'))]
    dot_general x4 -> x0, local copies, waits for them, and re-layouts: 7.44 us -> none  [against_rows(): lax.dot_general(left, right, (((1,), (1,)), ((), ())), preferred_element_...]
    all_to_all x3, waiting for transfers between devices: 19.6 us -> 26.4 us  [the longest x1 18.4 us: body(): lax.all_to_all(states, 'section', split_axis=0, concat_axis=1, tiled=True)]
  transfers between devices with their start and end apart: 4 -> 4, of which waited for: 2 -> 3; matrix products, arithmetic and copies ran while one was open for 7% -> 2% of each run, Pallas kernels for 0% -> 0%
where the time goes in v1:
time: 239 us; the launch traced here: 238 us
  waiting for transfers between devices  91 us (38%)
  Pallas kernels  57.5 us (24%)
  blocking collectives  45.7 us (19%)
  between operations  14.2 us (6%)
  starting transfers between devices  11.4 us (5%)
  local copies, waits for them, and re-layouts  10.5 us (4%)
  other arithmetic  8.05 us (3%)
    psum x1, waiting for transfers between devices, body(): summed = lax.psum(totals, ('section', 'dp'))  63.9 us
    pallas_call x1, Pallas kernels, local_part(): pl.pallas_call(compute_kernel, name='block_both_ways', in_specs=[hbm, hbm...  57.5 us
    psum x1, blocking collectives, body(): summed = lax.psum(totals, ('section', 'dp'))  45.7 us
    all_to_all x1, waiting for transfers between devices, body(): lax.all_to_all(states, 'section', split_axis=0, concat_axis=1, tiled=True)  18.4 us
    unnamed x23, local copies, waits for them, and re-layouts  9.7 us
    all_to_all x1, waiting for transfers between devices, body(): lax.all_to_all(embed.astype(bf16), 'section', split_axis=1, concat_axis=0...  8.01 us
  transfers between devices with their start and end apart: 4, of which 3 were waited for; matrix products, arithmetic and copies ran while one was open for 2% of the time, Pallas kernels for 0%

profile of v1, /device:TPU:0, one launch (start us, length us, event | category | flops | bytes accessed | tf_op | source)
XLA Modules:
  0.0 238.3 jit_solution(14469094626221116404)
XLA Ops:
  7.2 57.5 %block_both_ways.1 = (bf16[2,1,1024,256]{3,2,1,0:T(8,128)(2,1)}, f32[2,1,1024,256]{3,2,1,0:T(8,128)}, f32[256,768]{1,0:T(8,128)}, f32[256,256]{1,0:T(8,128)}, f3...) custom-call(bf16[2,1024,256]{2,1,0:T(8,128)(2,1)} %start_hbm.1, bf16[2,1024,256]{2,1,0:T(8,128)(2,1)} %emb_hbm.1, ...), custom_call_target="tpu_custom_call" | custom-call | tf_op jit(solution)/shard_map/block_both_ways/pallas_call | solution.py:316
  64.7 1.6 fusion
  66.3 0.8 copy.37
  67.1 0.5 broadcast
  67.7 3.8 %reduce = bf16[1024,256]{1,0:T(8,128)(2,1)S(1)} reduce(bf16[1024,1,256]{2,1,0:T(2,128)(2,1)S(1)} %bitcast.12, bf16[]{:T(256)} %broadcast), dimensions={1}, to_apply=%bitcast.10.reduce_sub_computation | reduce | bytes 1048578
  71.5 0.9 reshape.85
  72.4 4.2 %all-to-all-start.2 = ((bf16[2,2,65536]{2,1,0:T(2,128)(2,1)}), bf16[2,2,65536]{2,1,0:T(2,128)(2,1)S(1)}, u32[]{:S(2)}, u32[]{:S(2)}) async-start(bf16[2,2,65536]{2,1,0:T(2,128)(2,1)} %reshape.85), calls=%async_computation.2 | async-start | bytes 1048576 | tf_op jit(solution)/shard_map/all_to_all | solution.py:385
  76.6 0.0 all-reduce.4.cloned.1.call-start
  76.6 0.0 copy-start
  76.6 0.7 all-reduce.4.cloned.1.call-update
  77.3 8.0 %all-to-all-done.2 = bf16[2,2,65536]{2,1,0:T(2,128)(2,1)S(1)} async-done(((bf16[2,2,65536]{2,1,0:T(2,128)(2,1)}), bf16[2,2,65536]{2,1,0:T(2,128)(2,1)S(1)}, u32[]{:S(2)}, u32[]{:S(2)}) %all-to-all-start.2) | async-done | bytes 524320 | tf_op jit(solution)/shard_map/all_to_all | solution.py:385
  85.3 0.0 copy-start.1
  85.3 0.8 copy-done.1
  86.1 3.6 %all-to-all-start = ((bf16[2,1,1024,256]{3,2,1,0:T(8,128)(2,1)}), bf16[2,1,1024,256]{3,2,1,0:T(8,128)(2,1)S(1)}, u32[]{:S(2)}, u32[]{:S(2)}) async-start(bf16[2,1,1024,256]{3,2,1,0:T(8,128)(2,1)} %get-tuple-element.23), calls=%async_computation | async-start | bytes 2097152 | tf_op jit(solution)/shard_map/all_to_all | solution.py:381
  89.7 0.0 copy-done
  89.7 0.0 copy-start.6
  89.7 1.1 convert_element_type.37
  90.8 18.4 %all-to-all-done = bf16[2,1,1024,256]{3,2,1,0:T(8,128)(2,1)S(1)} async-done(((bf16[2,1,1024,256]{3,2,1,0:T(8,128)(2,1)}), bf16[2,1,1024,256]{3,2,1,0:T(8,128)(2,1)S(1)}, u32[]{:S(2)}, u32[]{:S(2)}) %all-to-all-start) | async-done | bytes 1048608 | tf_op jit(solution)/shard_map/all_to_all | solution.py:381
  109.2 3.6 %all-to-all-start.1 = ((bf16[2,1,1024,256]{3,2,1,0:T(8,128)(2,1)}), bf16[2,1,1024,256]{3,2,1,0:T(8,128)(2,1)S(1)}, u32[]{:S(2)}, u32[]{:S(2)}) async-start(bf16[2,1,1024,256]{3,2,1,0:T(8,128)(2,1)} %convert_element_type.37), calls=%async_computation.1 | async-start | bytes 2097152 | tf_op jit(solution)/shard_map/all_to_all | solution.py:382
  112.8 0.0 copy-done.6
  112.8 45.7 %all-reduce = (f32[256]{0:T(256)}, f32[256]{0:T(256)}, f32[256]{0:T(256)}, f32[256]{0:T(256)}, f32[256]{0:T(256)}, /*index=5*/f32[256]{0:T(256)}, f32[256]{0:T(256)}, f32[1024]{0:T(1024)}, f32[256]{0:T(256)}) all-reduce(f32[256]{0:T(256)S(1)} %get-tuple-element.50, ...), channel_id=1, replica_groups=mesh['section'=2,'dp'=16] {'section','dp'}, use_global_device_ids=true, to_apply=%region_1.0 | all-reduce | flops 3072 | bytes 24576 | tf_op jit(solution)/shard_map/psum | solution.py:388
  158.6 1.4 reshape.86
  160.0 1.0 copy.35
  161.0 0.0 all-to-all-done.1
  161.1 1.5 bitcast_convert_fusion
  162.5 63.9 %all-reduce.4.cloned.1.call-done = (f32[256,768]{1,0:T(8,128)}, f32[256,256]{1,0:T(8,128)}, f32[256,1024]{1,0:T(8,128)}, f32[1024,256]{1,0:T(8,128)}) async-done(((f32[256,768]{1,0:T(8,128)}, f32[256,256]{1,0:T(8,128)}, f32[256,1024]{1,0:T(8,128)}, f32[1024,256]{1,0:T(8,128)}), (f32[256,768]{1,0:T(8,128)}, f32[256,256]{1,0:T(8,128)}, f32[256,1024]{1,0:T(8,128)}, ...) | async-done | bytes 3145744 | tf_op jit(solution)/shard_map/psum | solution.py:388
  226.4 0.0 copy-start.4
  226.5 0.0 copy-start.5
  226.5 0.0 copy-start.3
  226.5 1.0 copy.43
  227.4 0.5 copy-done.4
  228.0 0.0 copy-start.2
  228.0 0.9 copy.44
  228.8 0.0 copy-done.5
  228.8 0.7 copy.45
  229.5 0.0 copy-done.3
  229.6 1.0 copy.46
  230.5 0.0 copy-done.2
  230.5 1.0 copy.47
  (3 shorter events, 0.0 us)
Async XLA Ops:
  72.4 12.9 %all-to-all-start.2 = ((bf16[2,2,65536]{2,1,0:T(2,128)(2,1)}), bf16[2,2,65536]{2,1,0:T(2,128)(2,1)S(1)}, u32[]{:S(2)}, u32[]{:S(2)}) async-start(bf16[2,2,65536]{2,1,0:T(2,128)(2,1)} %reshape.85), calls=%async_computation.2 | async-start | bytes 1048576 | tf_op jit(solution)/shard_map/all_to_all | solution.py:385
  76.6 149.9 %all-reduce.4.cloned.1.call-start = ((), (), s32[]{:S(2)}) async-start(), calls=%async_computation.3 | async-start | bytes 6291456 | tf_op jit(solution)/shard_map/psum | solution.py:388
  76.6 13.1 %copy-start = (f32[2,1,1024,256]{3,2,1,0:T(8,128)S(1)}, f32[2,1,1024,256]{3,2,1,0:T(8,128)}, u32[]{:S(2)}) copy-start(f32[2,1,1024,256]{3,2,1,0:T(8,128)} %get-tuple-element.24) | copy-start | bytes 6291460
  85.3 0.8 copy-start.1
  86.1 23.1 %all-to-all-start = ((bf16[2,1,1024,256]{3,2,1,0:T(8,128)(2,1)}), bf16[2,1,1024,256]{3,2,1,0:T(8,128)(2,1)S(1)}, u32[]{:S(2)}, u32[]{:S(2)}) async-start(bf16[2,1,1024,256]{3,2,1,0:T(8,128)(2,1)} %get-tuple-element.23), calls=%async_computation | async-start | bytes 2097152 | tf_op jit(solution)/shard_map/all_to_all | solution.py:381
  89.7 23.1 %copy-start.6 = (f32[8,3072]{1,0:T(8,128)S(1)}, f32[8,3072]{1,0:T(8,128)}, u32[]{:S(2)}) copy-start(f32[8,3072]{1,0:T(8,128)} %get-tuple-element.25) | copy-start | bytes 294916
  109.2 51.9 %all-to-all-start.1 = ((bf16[2,1,1024,256]{3,2,1,0:T(8,128)(2,1)}), bf16[2,1,1024,256]{3,2,1,0:T(8,128)(2,1)S(1)}, u32[]{:S(2)}, u32[]{:S(2)}) async-start(bf16[2,1,1024,256]{3,2,1,0:T(8,128)(2,1)} %convert_element_type.37), calls=%async_computation.1 | async-start | bytes 2097152 | tf_op jit(solution)/shard_map/all_to_all | solution.py:382
  226.4 1.5 copy-start.4
  226.5 2.4 %copy-start.5 = (f32[256,256]{1,0:T(8,128)S(1)}, f32[256,256]{1,0:T(8,128)}, u32[]{:S(2)}) copy-start(f32[256,256]{1,0:T(8,128)} %get-tuple-element.75) | copy-start | bytes 786436
  226.5 3.1 %copy-start.3 = (f32[256,1024]{1,0:T(8,128)S(1)}, f32[256,1024]{1,0:T(8,128)}, u32[]{:S(2)}) copy-start(f32[256,1024]{1,0:T(8,128)} %get-tuple-element.79) | copy-start | bytes 3145732
  228.0 2.6 %copy-start.2 = (f32[1024,256]{1,0:T(8,128)S(1)}, f32[1024,256]{1,0:T(8,128)}, u32[]{:S(2)}) copy-start(f32[1024,256]{1,0:T(8,128)} %get-tuple-element.81) | copy-start | bytes 3145732
Sparse Core Ops, SparseCore 0:
  84.4 141.9 all-reduce.3

commit v2 on v1

--- a/solution.py
+++ b/solution.py
@@ -64,23 +64,165 @@
 
 N1G, N1B, QB, VB, OB, N2G, N2B, DB, UB = (256 * i for i in range(9))
 SUMS = 256 * 12
+DOWN_AT, OUT_AT, BULK_ROWS = 2048, 4096, 4608
+SUMS_AT, TAIL_ROWS = 1536, 1568
+MESH = pl.DeviceIdType.MESH
 
 
 def compute_kernel(
+    far_count,
     start_hbm, emb_hbm, cot_hbm, seg_ref, pad_ref,
     g1_ref, b1_ref, wqkv_ref, qb_ref, vb_ref, wout_ref, ob_ref, g2_ref, b2_ref, wup_ref, ub_ref,
     wdown_ref, db_ref,
-    state_ref, grad_ref, gqkv_ref, gout_ref, gup_ref, gdown_ref, sums_ref,
-    start_v, emb_v, cot_v, qx, kx, xbuf, hat1, scale1, normed1, qa, qt, ka, va, expo, inverse,
-    outcome, hat2, scale2, normed2, active, slope, hgrad, branch, mgrad, dout, goa, gt,
-    dq, dkt, dvt, pgrad, gdown_t, in_sem,
+    states_hbm, grads_hbm, extra_hbm, bulk_hbm, tail_hbm,
+    start_v, emb_v, qx, kx, xbuf, hat1, scales, normed1, qa, qt, ka, va, expo, inverse,
+    outcome, hat2, normed2, active, slope, hgrad, branch, mgrad, grads, states, goa, gt,
+    dq, dkt, dvt, pgrad, gqkv, gout, gup, gdown, sums,
+    bulk, bulk_core, bulk_plane, bulk_far, bulk_all, tail, tail_core, tail_plane, tail_far, tail_all,
+    in_sem, swap_send, swap_recv, sum_send, sum_recv,
 ):
     length, width = xbuf.shape
     count = length // BLOCK
     part = lax.axis_index("section")
+    place = lax.axis_index("dp")
+    core, middle_bit, far = place % 2, (place // 2) % 2, place // 4
+    plane = 2 * part + middle_bit
+
+    swap_peer = (1 - part, place)
+    core_peer = (part, place + 1 - 2 * core)
+
+    def plane_peer(step):
+        there = (plane + step) % 4
+        return (there // 2, 4 * far + 2 * (there % 2) + core)
+
+    def far_peer(step):
+        return (part, 4 * ((far + step) % far_count) + 2 * middle_bit + core)
+
+    peers = [swap_peer, core_peer, plane_peer(1), plane_peer(3)]
+    peers += [far_peer(step) for step in range(1, far_count)]
+    barrier = pltpu.get_barrier_semaphore()
+    for peer in peers:
+        pl.semaphore_signal(barrier, inc=1, device_id=peer, device_id_type=MESH)
+
+    def remote(src, dst, sems, at, peer):
+        return pltpu.make_async_remote_copy(
+            src_ref=src, dst_ref=dst, send_sem=sems[0].at[at], recv_sem=sems[1].at[at],
+            device_id=peer, device_id_type=MESH,
+        )
+
+    class Sum:
+        def __init__(self, first_sem, own, by_core, by_plane, by_far, result):
+            self.own, self.by_core, self.by_plane, self.by_far = own, by_core, by_plane, by_far
+            self.result, self.first_sem = result, first_sem
+            self.half = own.shape[0] // 2
+            self.quarter = self.half // 4
+            self.piece = self.quarter // far_count
+            self.core_at = core * self.half
+            self.plane_at = self.core_at + plane * self.quarter
+            self.far_at = self.plane_at + far * self.piece
+
+        def rows(self, at, size):
+            return pl.ds(pl.multiple_of(at, 16), size)
+
+        def copy(self, at, src, dst, peer):
+            return remote(src, dst, (sum_send, sum_recv), self.first_sem + at, peer)
+
+        def core_out(self):
+            rows = self.rows((1 - core) * self.half, self.half)
+            return [self.copy(0, self.own.at[rows], self.by_core, core_peer)]
+
+        def plane_out(self):
+            copies = []
+            for step in range(1, 4):
+                there = (plane + step) % 4
+                rows = self.rows(self.core_at + there * self.quarter, self.quarter)
+                copies.append(
+                    self.copy(step, self.own.at[rows], self.by_plane.at[step - 1], plane_peer(step))
+                )
+            return copies
+
+        def far_out(self):
+            copies = []
+            for step in range(1, far_count):
+                there = (far + step) % far_count
+                rows = self.rows(self.plane_at + there * self.piece, self.piece)
+                copies.append(
+                    self.copy(3 + step, self.own.at[rows], self.by_far.at[step - 1], far_peer(step))
+                )
+            return copies
+
+        def far_back(self):
+            rows = self.rows(self.far_at, self.piece)
+            return [
+                self.copy(2 + far_count + step, self.result.at[rows], self.result.at[rows], far_peer(step))
+                for step in range(1, far_count)
+            ]
+
+        def plane_back(self):
+            rows = self.rows(self.plane_at, self.quarter)
+            return [
+                self.copy(1 + 2 * far_count + step, self.result.at[rows], self.result.at[rows], plane_peer(step))
+                for step in range(1, 4)
+            ]
+
+        def core_back(self):
+            rows = self.rows(self.core_at, self.half)
+            return [self.copy(5 + 2 * far_count, self.result.at[rows], self.result.at[rows], core_peer)]
+
+        def add_core(self):
+            step_rows = self.quarter
+
+            def add(i, _):
+                rows = self.rows(self.core_at + i * step_rows, step_rows)
+                theirs = self.rows(i * step_rows, step_rows)
+                self.own[rows, :] = (self.own[rows, :].astype(f32) + self.by_core[theirs, :].astype(f32)).astype(bf16)
+                return 0
+
+            lax.fori_loop(0, 4, add, 0)
+
+        def add_plane(self):
+            rows = self.rows(self.plane_at, self.quarter)
+            total = self.own[rows, :].astype(f32)
+            for step in range(3):
+                total = total + self.by_plane[step].astype(f32)
+            self.own[rows, :] = total.astype(bf16)
+
+        def add_far(self):
+            rows = self.rows(self.far_at, self.piece)
+            total = self.own[rows, :].astype(f32)
+            for step in range(far_count - 1):
+                total = total + self.by_far[step].astype(f32)
+            self.result[rows, :] = total.astype(bf16)
+
+    def start(copies):
+        for copy in copies:
+            copy.start()
+
+    def finish(copies):
+        for copy in copies:
+            copy.wait()
+
+    sum_bulk = Sum(0, bulk, bulk_core, bulk_plane, bulk_far, bulk_all)
+    sum_tail = Sum(6 + 2 * far_count, tail, tail_core, tail_plane, tail_far, tail_all)
+
+    def state_copy():
+        return remote(states.at[1 - part], states_hbm.at[part], (swap_send, swap_recv), 0, swap_peer)
+
+    def main_copy(t, b):
+        rows = slice(b * BLOCK, b * BLOCK + BLOCK)
+        return remote(grads.at[t, rows], grads_hbm.at[part, rows], (swap_send, swap_recv), 1 + b, swap_peer)
+
+    def extra_copy(t, b):
+        rows = slice(b * BLOCK, b * BLOCK + BLOCK)
+        there = b % (count // 2)
+        half_rows = slice(there * BLOCK, there * BLOCK + BLOCK)
+        return remote(
+            grads.at[t, rows], extra_hbm.at[part, half_rows], (swap_send, swap_recv), 1 + count + there, swap_peer
+        )
+
     loads = [
         pltpu.make_async_copy(hbm.at[part], dest, in_sem.at[i])
-        for i, (hbm, dest) in enumerate(((start_hbm, start_v), (emb_hbm, emb_v), (cot_hbm, cot_v)))
+        for i, (hbm, dest) in enumerate(((start_hbm, start_v), (emb_hbm, emb_v), (cot_hbm, grads.at[2])))
     ]
     for load in loads:
         load.start()
@@ -112,7 +254,7 @@
             hat, scale = normalise(xbuf[rows, :])
             normed = (hat * row_of(g1_ref) + row_of(b1_ref)).astype(bf16)
             hat1[t, rows, :] = hat
-            scale1[t, rows, :] = jnp.broadcast_to(scale, (BLOCK, 128))
+            scales[t, rows, 0:1] = scale
             normed1[t, rows, :] = normed
             q = (mul(normed, wqkv_ref[:, :width]) + row_of(qb_ref)).astype(bf16)
             q = q * jnp.asarray(HEAD_DIM**-0.5, bf16)
@@ -166,7 +308,7 @@
             hat, scale = normalise(middle)
             normed = (hat * row_of(g2_ref) + row_of(b2_ref)).astype(bf16)
             hat2[t, rows, :] = hat
-            scale2[t, rows, :] = jnp.broadcast_to(scale, (BLOCK, 128))
+            scales[t, rows, 1:2] = scale
             normed2[t, rows, :] = normed
             total = middle + row_of(db_ref)
             for c in range(wup_ref.shape[1] // 256):
@@ -179,7 +321,7 @@
                 slope[t, rows, columns] = (phi + hidden * density).astype(bf16)
                 total = total + mul(act, wdown_ref[columns, :])
             state = total.astype(bf16)
-            state_ref[t, 0, rows, :] = state
+            states[t, rows, :] = state
             xbuf[rows, :] = state.astype(f32) + emb_v[rows, :].astype(f32)
             return 0
 
@@ -188,23 +330,23 @@
 
     lax.fori_loop(0, 2, forward, 0)
 
-    sums_ref[...] = jnp.zeros_like(sums_ref)
-    gqkv_ref[...] = jnp.zeros_like(gqkv_ref)
-    gout_ref[...] = jnp.zeros_like(gout_ref)
-    gup_ref[...] = jnp.zeros_like(gup_ref)
-    gdown_t[...] = jnp.zeros_like(gdown_t)
-    dout[...] = cot_v[...]
+    for total in (sums, gqkv, gout, gup, gdown):
+        total[...] = jnp.zeros_like(total)
+    pl.semaphore_wait(barrier, len(peers))
+    state_copy().start()
+    keep_state = pltpu.make_async_copy(states.at[part], states_hbm.at[part], in_sem.at[0])
+    keep_state.start()
 
     def add_sums(at, values):
         columns = slice(at, at + values.shape[1])
-        sums_ref[:, columns] += eight_sums(values)
+        sums[:, columns] += eight_sums(values)
 
     def backward(step, _):
         t = 1 - step
 
         def feed_back(b, _):
             rows = rows_at(b)
-            down = dout[rows, :]
+            down = grads[t + 1, rows, :]
             down_wide = down.astype(f32)
             add_sums(DB, down_wide)
             cotangent = jnp.zeros((BLOCK, width), f32)
@@ -218,7 +360,7 @@
             hat = hat2[t, rows, :]
             add_sums(N2G, cotangent * hat)
             add_sums(N2B, cotangent)
-            middle = down_wide + norm_back(cotangent, row_of(g2_ref), hat, scale2[t, rows, 0:1])
+            middle = down_wide + norm_back(cotangent, row_of(g2_ref), hat, scales[t, rows, 1:2])
             mgrad[rows, :] = middle
             low = middle.astype(bf16)
             branch[rows, :] = low
@@ -242,12 +384,26 @@
 
         lax.fori_loop(0, count, feed_back, 0)
 
-        gdown_t[...] += mul_columns(dout[...], active[t])
-        gup_ref[...] += mul_columns(normed2[t], hgrad[...])
+        gdown[...] += mul_columns(grads[t + 1], active[t])
+        gup[...] += mul_columns(normed2[t], hgrad[...])
         for pair in range(HEADS // 2):
-            gout_ref[pair * 128 : pair * 128 + 128, :] += mul_columns(
+            gout[pair * 128 : pair * 128 + 128, :] += mul_columns(
                 outcome[t, pair].astype(bf16), branch[...]
             )
+
+        @pl.when(t == 0)
+        def _():
+            for i in range(wup_ref.shape[1] // 128):
+                lanes = slice(i * 128, i * 128 + 128)
+                bulk[i * width : (i + 1) * width, :] = gup[:, lanes].astype(bf16)
+                at = DOWN_AT + i * width
+                bulk[at : at + width, :] = gdown[:, lanes].astype(bf16)
+            for i in range(width // 128):
+                at = OUT_AT + i * width
+                bulk[at : at + width, :] = gout[:, i * 128 : i * 128 + 128].astype(bf16)
+            if bulk.shape[0] > BULK_ROWS:
+                bulk[BULK_ROWS:, :] = jnp.zeros((bulk.shape[0] - BULK_ROWS, 128), bf16)
+            start(sum_bulk.core_out())
 
         for b, first, store in reversed(blocks_of(length)[0]):
             rows = slice(b * BLOCK, b * BLOCK + BLOCK)
@@ -289,18 +445,145 @@
             hat = hat1[t, rows, :]
             add_sums(N1G, cotangent * hat)
             add_sums(N1B, cotangent)
-            x_grad = mgrad[rows, :] + norm_back(cotangent, row_of(g1_ref), hat, scale1[t, rows, 0:1])
-            grad_ref[t, 0, rows, :] = x_grad
-            dout[rows, :] = x_grad.astype(bf16)
-
-        gqkv_ref[...] += mul_columns(normed1[t], pgrad[...])
+            x_grad = mgrad[rows, :] + norm_back(cotangent, row_of(g1_ref), hat, scales[t, rows, 0:1])
+            grads[t, rows, :] = x_grad.astype(bf16)
+
+            @pl.when(part == 1 - t)
+            def _():
+                main_copy(t, b).start()
+
+            @pl.when((part == t) & (t == 1 - b // (count // 2)))
+            def _():
+                extra_copy(t, b).start()
+
+            if b == count - 1:
+                @pl.when(t == 0)
+                def _():
+                    finish(sum_bulk.core_out())
+                    sum_bulk.add_core()
+                    start(sum_bulk.plane_out())
+            if b == 0:
+                @pl.when(t == 0)
+                def _():
+                    finish(sum_bulk.plane_out())
+                    sum_bulk.add_plane()
+                    start(sum_bulk.far_out())
+
+        gqkv[...] += mul_columns(normed1[t], pgrad[...])
         return 0
 
     lax.fori_loop(0, 2, backward, 0)
-    gdown_ref[...] = gdown_t[...].T
-
-
-def local_part(args):
+
+    for i in range(3 * width // 128):
+        tail[i * width : (i + 1) * width, :] = gqkv[:, i * 128 : i * 128 + 128].astype(bf16)
+    total = jnp.sum(sums[...], axis=0, keepdims=True)
+    parts = [total[:, i * 128 : i * 128 + 128] for i in range(SUMS // 128)]
+    parts.append(jnp.zeros((8, 128), f32))
+    tail[SUMS_AT : SUMS_AT + 32, :] = jnp.concatenate(parts, axis=0).astype(bf16)
+    tail[SUMS_AT + 32 :, :] = jnp.zeros((tail.shape[0] - SUMS_AT - 32, 128), bf16)
+    start(sum_tail.core_out())
+    half_rows = pl.ds(pl.multiple_of(part * (length // 2), BLOCK), length // 2)
+    keep_grad = pltpu.make_async_copy(grads.at[part], grads_hbm.at[part], in_sem.at[1])
+    keep_extra = pltpu.make_async_copy(grads.at[1 - part, half_rows], extra_hbm.at[part], in_sem.at[2])
+    keep_grad.start()
+    keep_extra.start()
+    finish(sum_bulk.far_out())
+    sum_bulk.add_far()
+    start(sum_bulk.far_back())
+    finish(sum_tail.core_out())
+    sum_tail.add_core()
+    start(sum_tail.plane_out())
+    finish(sum_bulk.far_back())
+    start(sum_bulk.plane_back())
+    finish(sum_tail.plane_out())
+    sum_tail.add_plane()
+    start(sum_tail.far_out())
+    finish(sum_tail.far_out())
+    sum_tail.add_far()
+    start(sum_tail.far_back())
+    finish(sum_bulk.plane_back())
+    start(sum_bulk.core_back())
+    finish(sum_tail.far_back())
+    start(sum_tail.plane_back())
+    finish(sum_bulk.core_back())
+    keep_bulk = pltpu.make_async_copy(bulk_all, bulk_hbm, in_sem.at[3])
+    keep_bulk.start()
+    finish(sum_tail.plane_back())
+    start(sum_tail.core_back())
+    finish(sum_tail.core_back())
+    keep_tail = pltpu.make_async_copy(tail_all, tail_hbm, in_sem.at[4])
+    keep_tail.start()
+
+    state_copy().wait()
+    for b in range(count):
+        main_copy(0, b).wait()
+    for b in range(count // 2):
+        extra_copy(0, b).wait()
+    for keep in (keep_state, keep_grad, keep_extra, keep_bulk, keep_tail):
+        keep.wait()
+
+
+def padded(rows, devices):
+    unit = 16 * devices
+    return (rows + unit - 1) // unit * unit
+
+
+def finish_kernel(
+    states_hbm, grads_hbm, extra_hbm, bulk_hbm, tail_hbm,
+    loop_out, grad_out, embed_out, n1g, n1b, gqkv, qb, vb, gout, ob, n2g, n2b, gup, ub, gdown, db,
+    grads, extra, bulk, tail, grad_v, embed_v, gqkv_v, gout_v, gup_v, gdown_v, sems,
+):
+    part = lax.axis_index("section")
+    length, width = grads.shape[1:]
+
+    def copy(at, src, dst):
+        return pltpu.make_async_copy(src, dst, sems.at[at])
+
+    passed = copy(0, states_hbm, loop_out.at[0])
+    loads = [copy(1, grads_hbm, grads), copy(2, extra_hbm, extra), copy(3, bulk_hbm, bulk), copy(4, tail_hbm, tail)]
+    passed.start()
+    for load in loads:
+        load.start()
+    loads[0].wait()
+    grad_v[...] = grads[...].astype(f32)
+    stores = [copy(5, grad_v, grad_out.at[0])]
+    stores[-1].start()
+    loads[1].wait()
+    half_rows = pl.ds(pl.multiple_of(part * (length // 2), BLOCK), length // 2)
+    embed_v[...] = grads[:, half_rows, :].astype(f32) + extra[...].astype(f32)
+    stores.append(copy(6, embed_v, embed_out))
+    stores[-1].start()
+    loads[2].wait()
+    for i in range(gup_v.shape[1] // 128):
+        lanes = slice(i * 128, i * 128 + 128)
+        gup_v[:, lanes] = bulk[i * width : (i + 1) * width, :].astype(f32)
+    stores.append(copy(7, gup_v, gup))
+    stores[-1].start()
+    for i in range(gup_v.shape[1] // 128):
+        at = DOWN_AT + i * width
+        gdown_v[i * 128 : i * 128 + 128, :] = bulk[at : at + width, :].T.astype(f32)
+    stores.append(copy(8, gdown_v, gdown))
+    stores[-1].start()
+    for i in range(width // 128):
+        at = OUT_AT + i * width
+        gout_v[:, i * 128 : i * 128 + 128] = bulk[at : at + width, :].astype(f32)
+    stores.append(copy(9, gout_v, gout))
+    stores[-1].start()
+    loads[3].wait()
+    for i in range(3 * width // 128):
+        gqkv_v[:, i * 128 : i * 128 + 128] = tail[i * width : (i + 1) * width, :].astype(f32)
+    stores.append(copy(10, gqkv_v, gqkv))
+    stores[-1].start()
+    small = tail[SUMS_AT : SUMS_AT + 32, :].astype(f32)
+    for at, ref in ((N1G, n1g), (N1B, n1b), (QB, qb), (VB, vb), (OB, ob), (N2G, n2g), (N2B, n2b), (DB, db), (UB, ub)):
+        for i in range(ref.shape[0] // 128):
+            ref[i * 128 : i * 128 + 128] = small[at // 128 + i]
+    passed.wait()
+    for store in stores:
+        store.wait()
+
+
+def whole_block(sections, places, *args):
     start = args[0]
     _, length, width = start.shape
     hidden = args[15].shape[0]
@@ -309,26 +592,39 @@
     hbm = pl.BlockSpec(memory_space=pl.ANY)
     count = length // BLOCK
     pairs = HEADS // 2
+    devices = sections * places
+    far_count = places // 4
+    bulk_rows, tail_rows = padded(BULK_ROWS, devices), padded(TAIL_ROWS, devices)
 
     def V(*shape, dtype=bf16):
         return pltpu.VMEM(shape, dtype)
 
-    return pl.pallas_call(
-        compute_kernel,
+    def O(*shape, dtype=f32):
+        return jax.ShapeDtypeStruct(shape, dtype)
+
+    def sum_buffers(rows):
+        return [
+            V(rows, 128),
+            V(rows // 2, 128),
+            V(3, rows // 8, 128),
+            V(far_count - 1, rows // devices, 128),
+            V(rows, 128),
+        ]
+
+    copies = 2 * (6 + 2 * far_count)
+    between = pl.pallas_call(
+        partial(compute_kernel, far_count),
         name="block_both_ways",
         in_specs=[hbm, hbm, hbm, vmem, smem] + [vmem] * 13,
-        out_specs=[vmem] * 7,
+        out_specs=[hbm] * 5,
         out_shape=[
-            jax.ShapeDtypeStruct((2, 1, length, width), bf16),
-            jax.ShapeDtypeStruct((2, 1, length, width), f32),
-            jax.ShapeDtypeStruct((width, 3 * width), f32),
-            jax.ShapeDtypeStruct((width, width), f32),
-            jax.ShapeDtypeStruct((width, hidden), f32),
-            jax.ShapeDtypeStruct((hidden, width), f32),
-            jax.ShapeDtypeStruct((8, SUMS), f32),
+            O(2, length, width, dtype=bf16),
+            O(2, length, width, dtype=bf16),
+            O(2, length // 2, width, dtype=bf16),
+            O(bulk_rows, 128, dtype=bf16),
+            O(tail_rows, 128, dtype=bf16),
         ],
         scratch_shapes=[
-            V(length, width),
             V(length, width),
             V(length, width),
             V(length, 128),
@@ -345,54 +641,72 @@
             V(2, pairs, length, 128, dtype=f32),
             V(2, pairs, length, 128, dtype=f32),
             V(2, length, width, dtype=f32),
-            V(2, length, 128, dtype=f32),
             V(2, length, width),
             V(2, length, hidden),
             V(2, length, hidden),
             V(length, hidden),
             V(length, width),
             V(length, width, dtype=f32),
-            V(length, width),
+            V(3, length, width),
+            V(2, length, width),
             V(HEADS, length, 128),
             V(width, length),
             V(pairs, BLOCK, 128, dtype=f32),
             V(width, length, dtype=f32),
             V(width, length, dtype=f32),
             V(length, 3 * width),
+            V(width, 3 * width, dtype=f32),
+            V(width, width, dtype=f32),
             V(width, hidden, dtype=f32),
-            pltpu.SemaphoreType.DMA((3,)),
+            V(width, hidden, dtype=f32),
+            V(8, SUMS, dtype=f32),
+        ]
+        + sum_buffers(bulk_rows)
+        + sum_buffers(tail_rows)
+        + [
+            pltpu.SemaphoreType.DMA((5,)),
+            pltpu.SemaphoreType.DMA((1 + count + count // 2,)),
+            pltpu.SemaphoreType.DMA((1 + count + count // 2,)),
+            pltpu.SemaphoreType.DMA((copies,)),
+            pltpu.SemaphoreType.DMA((copies,)),
         ],
-        compiler_params=pltpu.CompilerParams(vmem_limit_bytes=60 << 20),
+        compiler_params=pltpu.CompilerParams(
+            vmem_limit_bytes=63 << 20, collective_id=0, has_side_effects=True
+        ),
     )(*args)
-
-
-def body(*args):
-    states, grads, gqkv, gout, gup, gdown, sums = local_part(args)
-    sums = jnp.sum(sums, axis=0)
-
-    def piece(at, size=256):
-        return sums[at : at + size]
-
-    totals = (
-        piece(N1G), piece(N1B), gqkv, piece(QB), piece(VB), gout, piece(OB), piece(N2G), piece(N2B),
-        gup, piece(UB, 1024), gdown, piece(DB),
-    )
-    embed = grads[0] + grads[1]
-    loop_states = lax.all_to_all(states, "section", split_axis=0, concat_axis=1, tiled=True)
-    state_grads = lax.all_to_all(
-        grads.astype(bf16), "section", split_axis=0, concat_axis=1, tiled=True
-    ).astype(f32)
-    embed_grad = lax.all_to_all(
-        embed.astype(bf16), "section", split_axis=1, concat_axis=0, tiled=True
-    ).astype(f32)
-    summed = lax.psum(totals, ("section", "dp"))
-    return (loop_states, state_grads, embed_grad) + tuple(summed)
+    return pl.pallas_call(
+        finish_kernel,
+        name="widen",
+        in_specs=[hbm] * 5,
+        out_specs=[hbm, hbm, hbm, vmem, vmem, hbm, vmem, vmem, hbm, vmem, vmem, vmem, hbm, vmem, hbm, vmem],
+        out_shape=[
+            O(1, 2, length, width, dtype=bf16),
+            O(1, 2, length, width),
+            O(2, length // 2, width),
+            O(width), O(width), O(width, 3 * width), O(width), O(width), O(width, width), O(width),
+            O(width), O(width), O(width, hidden), O(hidden), O(hidden, width), O(width),
+        ],
+        scratch_shapes=[
+            V(2, length, width),
+            V(2, length // 2, width),
+            V(bulk_rows, 128),
+            V(tail_rows, 128),
+            V(2, length, width, dtype=f32),
+            V(2, length // 2, width, dtype=f32),
+            V(width, 3 * width, dtype=f32),
+            V(width, width, dtype=f32),
+            V(width, hidden, dtype=f32),
+            V(hidden, width, dtype=f32),
+            pltpu.SemaphoreType.DMA((11,)),
+        ],
+        compiler_params=pltpu.CompilerParams(vmem_limit_bytes=32 << 20),
+    )(*between)
 
 
 def solution(mesh):
     rows = P("dp", None, None)
     return jax.shard_map(
-        body,
+        partial(whole_block, mesh.shape["section"], mesh.shape["dp"]),
         mesh=mesh,
         in_specs=(rows, rows, rows, P("dp", None), P("dp")) + (P(),) * 13,
         out_specs=(

time: 239 us -> 101 us (0.42)
  waiting for transfers between devices: 91 us -> 0 us
  blocking collectives: 45.7 us -> 0 us
  Pallas kernels: 57.5 us -> 94 us
  between operations: 14.2 us -> 0.67 us
  starting transfers between devices: 11.4 us -> 0 us
  other arithmetic: 8.05 us -> 0 us
  local copies, waits for them, and re-layouts: 10.5 us -> 5.79 us
    psum x1 -> x0, waiting for transfers between devices: 63.9 us -> none  [body(): summed = lax.psum(totals, ('section', 'dp'))]
    psum x1 -> x0, blocking collectives: 45.7 us -> none  [body(): summed = lax.psum(totals, ('section', 'dp'))]
    pallas_call x1 -> x2, Pallas kernels: 57.5 us -> 94 us  [the longest x1 90.1 us: whole_block(): pl.pallas_call(partial(compute_kernel, far_count), name='block_both_ways'...]
    all_to_all x3 -> x0, waiting for transfers between devices: 26.4 us -> none  [the longest x1 18.4 us: body(): lax.all_to_all(states, 'section', split_axis=0, concat_axis=1, tiled=True)]
    all_to_all x3 -> x0, starting transfers between devices: 11.4 us -> none  [the longest x1 4.2 us: body(): lax.all_to_all(embed.astype(bf16), 'section', split_axis=1, concat_axis=0...]
    convert_element_type x3 -> x0, other arithmetic: 4.2 us -> none  [the longest x1 1.65 us: body(): embed.astype(bf16)]
    unnamed x23 -> x10, local copies, waits for them, and re-layouts: 9.7 us -> 5.79 us
    unnamed x1 -> x0, other arithmetic: 3.82 us -> none
  transfers between devices with their start and end apart: 4 -> 0, of which waited for: 3 -> 0; matrix products, arithmetic and copies ran while one was open for 2% -> 0% of each run, Pallas kernels for 0% -> 0%
where the time goes in v2:
time: 101 us; the launch traced here: 100 us
  Pallas kernels  94 us (93%)
  local copies, waits for them, and re-layouts  5.79 us (6%)
    pallas_call x1, Pallas kernels, whole_block(): pl.pallas_call(partial(compute_kernel, far_count), name='block_both_ways'...  90.1 us
    unnamed x10, local copies, waits for them, and re-layouts  5.79 us
    pallas_call x1, Pallas kernels, whole_block(): pl.pallas_call(finish_kernel, name='widen', in_specs=[hbm] * 5, out_specs...  3.87 us

profile of v2, /device:TPU:0, one launch (start us, length us, event | category | flops | bytes accessed | tf_op | source)
XLA Modules:
  0.0 100.4 jit_solution(15740018086205154265)
XLA Ops:
  0.7 90.1 %block_both_ways.1 = (bf16[2,1024,256]{2,1,0:T(8,128)(2,1)}, bf16[2,1024,256]{2,1,0:T(8,128)(2,1)}, bf16[2,512,256]{2,1,0:T(8,128)(2,1)}, bf16[4608,128]{1,0:T(8,128)(2,1)}, bf16[2048,128]{1,0:T(8,128)(2,1)}) custom-call(bf16[2,1024,256]{2,1,0:T(8,128)(2,1)} %start_hbm.1, bf16[2,1024,256]{2,1,0:T(8,128)(2,1)} %emb_hbm.1, bf16[2,1024,256]{2,1,0:T(8,128)(2,1)} %cot_hbm.1, ...), custom_call_target="tpu_custom_call" | custom-call | tf_op jit(solution)/shard_map/block_both_ways/pallas_call | solution.py:615
  90.8 0.0 copy-start
  90.8 1.3 %copy-done = bf16[4608,128]{1,0:T(8,128)(2,1)S(1)} copy-done((bf16[4608,128]{1,0:T(8,128)(2,1)S(1)}, bf16[4608,128]{1,0:T(8,128)(2,1)}, u32[]{:S(2)}) %copy-start) | copy-done | bytes 1179672
  92.0 0.0 copy-start.1
  92.0 1.2 %copy-done.1 = bf16[2,1024,256]{2,1,0:T(8,128)(2,1)S(1)} copy-done((bf16[2,1024,256]{2,1,0:T(8,128)(2,1)S(1)}, bf16[2,1024,256]{2,1,0:T(8,128)(2,1)}, u32[]{:S(2)}) %copy-start.1) | copy-done | bytes 1048600
  93.3 0.0 copy-start.2
  93.3 1.2 %copy-done.2 = bf16[2,1024,256]{2,1,0:T(8,128)(2,1)S(1)} copy-done((bf16[2,1024,256]{2,1,0:T(8,128)(2,1)S(1)}, bf16[2,1024,256]{2,1,0:T(8,128)(2,1)}, u32[]{:S(2)}) %copy-start.2) | copy-done | bytes 1048600
  94.5 0.0 copy-start.3
  94.5 1.0 %copy-done.3 = bf16[2,512,256]{2,1,0:T(8,128)(2,1)S(1)} copy-done((bf16[2,512,256]{2,1,0:T(8,128)(2,1)S(1)}, bf16[2,512,256]{2,1,0:T(8,128)(2,1)}, u32[]{:S(2)}) %copy-start.3) | copy-done | bytes 524312
  95.5 0.0 copy-start.4
  95.5 1.0 %copy-done.4 = bf16[2048,128]{1,0:T(8,128)(2,1)S(1)} copy-done((bf16[2048,128]{1,0:T(8,128)(2,1)S(1)}, bf16[2048,128]{1,0:T(8,128)(2,1)}, u32[]{:S(2)}) %copy-start.4) | copy-done | bytes 524312
  96.6 3.9 %widen.1 = (bf16[1,2,1024,256]{3,2,1,0:T(8,128)(2,1)}, f32[1,2,1024,256]{3,2,1,0:T(8,128)}, f32[2,512,256]{2,1,0:T(8,128)}, f32[256]{0:T(256)}, f32[256]{0:T(256...) custom-call(bf16[2,1024,256]{2,1,0:T(8,128)(2,1)S(1)} %copy-done.1, ...), custom_call_target="tpu_custom_call" | custom-call | tf_op jit(solution)/shard_map/widen/pallas_call | solution.py:677
Async XLA Ops:
  90.8 1.3 %copy-start = (bf16[4608,128]{1,0:T(8,128)(2,1)S(1)}, bf16[4608,128]{1,0:T(8,128)(2,1)}, u32[]{:S(2)}) copy-start(bf16[4608,128]{1,0:T(8,128)(2,1)} %get-tuple-element.24.bulk_hbm) | copy-start | bytes 3538948
  92.0 1.2 %copy-start.1 = (bf16[2,1024,256]{2,1,0:T(8,128)(2,1)S(1)}, bf16[2,1024,256]{2,1,0:T(8,128)(2,1)}, u32[]{:S(2)}) copy-start(bf16[2,1024,256]{2,1,0:T(8,128)(2,1)} %get-tuple-element.21.states_hbm) | copy-start | bytes 3145732
  93.3 1.2 %copy-start.2 = (bf16[2,1024,256]{2,1,0:T(8,128)(2,1)S(1)}, bf16[2,1024,256]{2,1,0:T(8,128)(2,1)}, u32[]{:S(2)}) copy-start(bf16[2,1024,256]{2,1,0:T(8,128)(2,1)} %get-tuple-element.22.grads_hbm) | copy-start | bytes 3145732
  94.5 1.0 %copy-start.3 = (bf16[2,512,256]{2,1,0:T(8,128)(2,1)S(1)}, bf16[2,512,256]{2,1,0:T(8,128)(2,1)}, u32[]{:S(2)}) copy-start(bf16[2,512,256]{2,1,0:T(8,128)(2,1)} %get-tuple-element.23.extra_hbm) | copy-start | bytes 1572868
  95.5 1.0 %copy-start.4 = (bf16[2048,128]{1,0:T(8,128)(2,1)S(1)}, bf16[2048,128]{1,0:T(8,128)(2,1)}, u32[]{:S(2)}) copy-start(bf16[2048,128]{1,0:T(8,128)(2,1)} %get-tuple-element.25.tail_hbm) | copy-start | bytes 1572868

commit v3 on v2

v3 whole, which is shorter than its diff:
```python
from functools import partial

import jax
import jax.numpy as jnp
from jax import lax
from jax.experimental import pallas as pl
from jax.experimental.pallas import tpu as pltpu
from jax.sharding import PartitionSpec as P

HEADS = 4
HEAD_DIM = 64
BLOCK = 256
SPAN = 512
norm_eps = 1e-05
masked_score = -1e30
bf16 = jnp.bfloat16
f32 = jnp.float32


def mul(left, right):
    return jnp.dot(left, right, preferred_element_type=f32)


def mul_rows(left, right):
    return lax.dot_general(left, right, (((1,), (1,)), ((), ())), preferred_element_type=f32)


def mul_columns(left, right):
    return lax.dot_general(left, right, (((0,), (0,)), ((), ())), preferred_element_type=f32)


def row_of(ref):
    return ref[...].reshape(1, ref.shape[0])


def eight_sums(values):
    rows, width = values.shape
    return jnp.sum(values.reshape(rows // 8, 8, width), axis=0)


def normalise(x):
    average = jnp.mean(x, axis=-1, keepdims=True)
    centred = x - average
    spread = jnp.mean(centred * centred, axis=-1, keepdims=True)
    scale = lax.rsqrt(spread + norm_eps)
    return centred * scale, scale


def norm_back(cotangent, gain, hat, scale):
    scaled = cotangent * gain
    first = jnp.mean(scaled, axis=-1, keepdims=True)
    second = jnp.mean(scaled * hat, axis=-1, keepdims=True)
    return scale * (scaled - first - hat * second)


def blocks_of(length):
    result, store = [], 0
    for b in range(length // BLOCK):
        first = max(0, b - SPAN // BLOCK)
        result.append((b, first, store))
        store += (b + 1 - first) * BLOCK
    return result, store


def reach(half, distance, wide):
    low = 128 if half == 1 and distance == SPAN // BLOCK else 0
    return low, wide - (128 if half == 0 else 0)


N1G, N1B, QB, VB, OB, N2G, N2B, DB, UB = (256 * i for i in range(9))
SUMS = 256 * 12
DOWN_ROWS, OUT_AT, UP_ROWS, QKV_ROWS = 2048, 2048, 2560, 1536
MESH = pl.DeviceIdType.MESH


def compute_kernel(
    far_count,
    start_hbm, emb_hbm, cot_hbm, seg_ref, pad_ref,
    g1_ref, b1_ref, wqkv_ref, qb_ref, vb_ref, wout_ref, ob_ref, g2_ref, b2_ref, wup_ref, ub_ref,
    wdown_ref, db_ref,
    states_hbm, grads_hbm, extra_hbm, down_hbm, up_hbm, qkv_hbm, small_hbm,
    start_v, emb_v, kx, wq_t, qb_t, edge, score_a, score_b, slope_a, slope_b,
    xbuf, hat1, scales, normed1, qa, ka, kt, va, vt, expo, inverse,
    outcome, hat2, normed2, active, slope, hgrad, branch, mgrad, grads, states, goa,
    dkt, dvt, pgrad, gqkv, gout, gup, gdown, sums, qv_sums,
    down, down_core, down_plane, down_far, down_all,
    up, up_core, up_plane, up_far, up_all,
    qkv, qkv_core, qkv_chip, qkv_all,
    small, small_there, in_sem, swap_send, swap_recv, sum_send, sum_recv,
):
    length, width = xbuf.shape
    count = length // BLOCK
    part = lax.axis_index("section")
    place = lax.axis_index("dp")
    core, near, far = place % 2, (place // 2) % 2, place // 4

    across_peer = (1 - part, place)
    core_peer = (part, place + 1 - 2 * core)
    near_peer = (part, place + 2 - 4 * near)

    plane = 2 * part + near

    def plane_peer(step):
        there = (plane + step) % 4
        return (there // 2, 4 * far + 2 * (there % 2) + core)

    def far_peer(step):
        return (part, 4 * ((far + step) % far_count) + 2 * near + core)

    chips = lax.axis_size("section") * lax.axis_size("dp") // 2
    chip = part * (chips // 2) + place // 2

    def chip_peer(step):
        there = (chip + step) % chips
        return (there // (chips // 2), 2 * (there % (chips // 2)) + core)

    peers = [core_peer] + [chip_peer(step) for step in range(1, chips)]
    barrier = pltpu.get_barrier_semaphore()
    for peer in peers:
        pl.semaphore_signal(barrier, inc=1, device_id=peer, device_id_type=MESH)

    def remote(src, dst, sems, at, peer):
        return pltpu.make_async_remote_copy(
            src_ref=src, dst_ref=dst, send_sem=sems[0].at[at], recv_sem=sems[1].at[at],
            device_id=peer, device_id_type=MESH,
        )

    class Sum:
        def __init__(self, first_sem, own, by_core, by_plane, by_far, result, result_hbm):
            self.first_sem, self.own, self.result = first_sem, own, result
            self.by_core, self.by_plane, self.by_far = by_core, by_plane, by_far
            half = own.shape[0] // 2
            quarter = half // 4
            piece = quarter // far_count
            core_at = core * half
            plane_at = core_at + plane * quarter
            self.sizes = (half, quarter, piece)
            self.starts = (core_at, plane_at, plane_at + far * piece)
            self.keep = pltpu.make_async_copy(result, result_hbm, in_sem.at[4 + (first_sem > 0)])
            self.stage = 0

        def rows(self, at, size):
            return pl.ds(pl.multiple_of(at, 16), size)

        def copy(self, at, src, dst, peer):
            return remote(src, dst, (sum_send, sum_recv), self.first_sem + at, peer)

        def out(self, level):
            if level == 0:
                rows = self.rows((1 - core) * self.sizes[0], self.sizes[0])
                return [self.copy(0, self.own.at[rows], self.by_core, core_peer)]
            copies = []
            size = self.sizes[level]
            if level == 1:
                for step in range(1, 4):
                    rows = self.rows(self.starts[0] + (plane + step) % 4 * size, size)
                    copies.append(self.copy(step, self.own.at[rows], self.by_plane.at[step - 1], plane_peer(step)))
            else:
                for step in range(1, far_count):
                    rows = self.rows(self.starts[1] + (far + step) % far_count * size, size)
                    copies.append(self.copy(3 + step, self.own.at[rows], self.by_far.at[step - 1], far_peer(step)))
            return copies

        def back(self, level):
            src = self.result.at[self.rows(self.starts[level], self.sizes[level])]
            first = 2 + far_count
            if level == 2:
                return [self.copy(first + step, src, src, far_peer(step)) for step in range(1, far_count)]
            if level == 1:
                return [self.copy(first + far_count - 1 + step, src, src, plane_peer(step)) for step in range(1, 4)]
            return [self.copy(first + far_count + 3, src, src, core_peer)]

        def add(self, level):
            rows = self.rows(self.starts[level], self.sizes[level])
            total = self.own[rows, :].astype(f32)
            if level == 0:
                total = total + self.by_core[...].astype(f32)
            else:
                others = self.by_plane if level == 1 else self.by_far
                for step in range(others.shape[0]):
                    total = total + others[step].astype(f32)
            target = self.result if level == 2 else self.own
            target[rows, :] = total.astype(bf16)

        def step(self):
            stage = self.stage
            self.stage += 1
            if 1 <= stage <= 3:
                finish(self.out(stage - 1))
                self.add(stage - 1)
            if stage >= 4:
                finish(self.back(6 - stage))
            if stage <= 2:
                start(self.out(stage))
            elif stage <= 5:
                start(self.back(5 - stage))
            else:
                self.keep.start()

    class ShortSum:
        def __init__(self, first_sem, own, by_core, by_chip, result, result_hbm):
            self.first_sem, self.own, self.result = first_sem, own, result
            self.by_core, self.by_chip = by_core, by_chip
            self.half = own.shape[0] // 2
            self.piece = self.half // chips
            self.core_at = core * self.half
            self.chip_at = self.core_at + chip * self.piece
            self.keep = pltpu.make_async_copy(result, result_hbm, in_sem.at[6])
            self.stage = 0

        def rows(self, at, size):
            return pl.ds(pl.multiple_of(at, 16), size)

        def copy(self, at, src, dst, peer):
            return remote(src, dst, (sum_send, sum_recv), self.first_sem + at, peer)

        def core_out(self):
            rows = self.rows((1 - core) * self.half, self.half)
            return [self.copy(0, self.own.at[rows], self.by_core, core_peer)]

        def chip_out(self):
            copies = []
            for step in range(1, chips):
                rows = self.rows(self.core_at + (chip + step) % chips * self.piece, self.piece)
                copies.append(self.copy(step, self.own.at[rows], self.by_chip.at[step - 1], chip_peer(step)))
            return copies

        def chip_back(self):
            src = self.result.at[self.rows(self.chip_at, self.piece)]
            return [self.copy(chips - 1 + step, src, src, chip_peer(step)) for step in range(1, chips)]

        def core_back(self):
            src = self.result.at[self.rows(self.core_at, self.half)]
            return [self.copy(2 * chips - 1, src, src, core_peer)]

        def step(self):
            stage = self.stage
            self.stage += 1
            if stage == 0:
                start(self.core_out())
            elif stage == 1:
                finish(self.core_out())
                rows = self.rows(self.core_at, self.half)
                total = self.own[rows, :].astype(f32) + self.by_core[...].astype(f32)
                self.own[rows, :] = total.astype(bf16)
                start(self.chip_out())
            elif stage == 2:
                finish(self.chip_out())
                rows = self.rows(self.chip_at, self.piece)
                total = self.own[rows, :].astype(f32)
                for step in range(chips - 1):
                    total = total + self.by_chip[step].astype(f32)
                self.result[rows, :] = total.astype(bf16)
                start(self.chip_back())
            elif stage == 3:
                finish(self.chip_back())
                start(self.core_back())
            else:
                finish(self.core_back())
                self.keep.start()

    class Small:
        def __init__(self, first_sem):
            self.first_sem, self.stage = first_sem, 0
            self.keep = pltpu.make_async_copy(small, small_hbm, in_sem.at[3])

        def copies(self, level):
            first = (0, 1, 2, 1 + far_count)[level]
            peers = ([core_peer], [near_peer], [far_peer(step) for step in range(1, far_count)], [across_peer])[level]
            return [
                remote(small, small_there.at[first + i], (sum_send, sum_recv), self.first_sem + first + i, peer)
                for i, peer in enumerate(peers)
            ]

        def step(self):
            stage = self.stage
            self.stage += 1
            if stage > 0:
                copies = self.copies(stage - 1)
                finish(copies)
                first = (0, 1, 2, 1 + far_count)[stage - 1]
                total = small[...]
                for i in range(len(copies)):
                    total = total + small_there[first + i]
                small[...] = total
            if stage < 4:
                start(self.copies(stage))
            else:
                self.keep.start()

    def start(copies):
        for copy in copies:
            copy.start()

    def finish(copies):
        for copy in copies:
            copy.wait()

    sems = 6 + 2 * far_count
    sum_down = Sum(0, down, down_core, down_plane, down_far, down_all, down_hbm)
    sum_up = Sum(sems, up, up_core, up_plane, up_far, up_all, up_hbm)
    sum_qkv = ShortSum(2 * sems, qkv, qkv_core, qkv_chip, qkv_all, qkv_hbm)
    sum_small = Small(2 * sems + 2 * chips)

    def pack(target, at, source):
        height = source.shape[0]
        for i in range(source.shape[1] // 128):
            target[at + i * height : at + (i + 1) * height, :] = source[:, i * 128 : i * 128 + 128].astype(bf16)

    def clear(target, used):
        if target.shape[0] > used:
            target[used:, :] = jnp.zeros((target.shape[0] - used, 128), bf16)

    def state_copy():
        return remote(states.at[1 - part], states_hbm.at[part], (swap_send, swap_recv), 0, across_peer)

    def main_copy(t, b):
        rows = slice(b * BLOCK, b * BLOCK + BLOCK)
        return remote(grads.at[t, rows], grads_hbm.at[part, rows], (swap_send, swap_recv), 1 + b, across_peer)

    def extra_copy(t, b):
        rows = slice(b * BLOCK, b * BLOCK + BLOCK)
        there = b % (count // 2)
        half_rows = slice(there * BLOCK, there * BLOCK + BLOCK)
        return remote(
            grads.at[t, rows], extra_hbm.at[part, half_rows], (swap_send, swap_recv), 1 + count + there, across_peer
        )

    loads = [
        pltpu.make_async_copy(hbm.at[part], dest, in_sem.at[i])
        for i, (hbm, dest) in enumerate(((start_hbm, start_v), (emb_hbm, emb_v), (cot_hbm, grads.at[2])))
    ]
    for load in loads:
        load.start()

    lane = lax.broadcasted_iota(jnp.int32, (128, 128), 1) & 63
    ids = jnp.where(part == 0, seg_ref[0:1, :], seg_ref[1:2, :])
    for c in range(length // 128):
        tokens = slice(c * 128, c * 128 + 128)
        turned = jnp.broadcast_to(ids[:, tokens].astype(f32), (128, 128)).T.astype(jnp.int32)
        kx[tokens, :] = jnp.where(turned == lane, 1.0, 0.0).astype(bf16)
    code = lax.broadcasted_iota(jnp.int32, (16, length), 0)
    unlike = jnp.where((code < 8) & (code != ids), masked_score, 0.0).astype(bf16)
    for h in range(HEADS):
        spare = 64 - h % 2 * 64
        for t in range(2):
            qa[t, h, spare : spare + 64, :] = jnp.zeros((64, length), bf16)
            qa[t, h, spare : spare + 16, :] = unlike
        goa[h, spare : spare + 64, :] = jnp.zeros((64, length), bf16)
        vt[h, 64:80, :] = jnp.ones((16, length), bf16)
    key_at = lax.broadcasted_iota(jnp.int32, (128, 128), 0)
    query_at = lax.broadcasted_iota(jnp.int32, (128, 128), 1)
    edge[0] = jnp.where(key_at <= query_at, 0.0, masked_score)
    live = key_at + (length - 128) < length - pad_ref[part]
    edge[1] = jnp.where((key_at == query_at) | ((key_at < query_at) & live), 0.0, masked_score)
    wq_t[...] = wqkv_ref[:, :width].T
    qb_t[...] = jnp.broadcast_to(row_of(qb_ref), (128, width)).T

    for load in loads:
        load.wait()
    xbuf[...] = start_v[...].astype(f32) + emb_v[...].astype(f32)

    low_half = lax.broadcasted_iota(jnp.int32, (BLOCK, 128), 1) < 64
    ones = jnp.ones((BLOCK, 128), bf16)

    def rows_at(b):
        return pl.ds(pl.multiple_of(b * BLOCK, BLOCK), BLOCK)

    def forward(t, _):
        def project(b, _):
            rows = rows_at(b)
            hat, scale = normalise(xbuf[rows, :])
            normed = (hat * row_of(g1_ref) + row_of(b1_ref)).astype(bf16)
            hat1[t, rows, :] = hat
            scales[t, rows, 0:1] = scale
            normed1[t, rows, :] = normed
            bias = jnp.concatenate([qb_t[...], qb_t[...]], axis=1)
            q = (mul_rows(wq_t[...], normed) + bias).astype(bf16) * jnp.asarray(HEAD_DIM**-0.5, bf16)
            k = mul(normed, wqkv_ref[:, width : 2 * width]).astype(bf16)
            v = (mul(normed, wqkv_ref[:, 2 * width :]) + row_of(vb_ref)).astype(bf16)
            kt[t, :, rows] = k.T
            turned = v.T
            for h in range(HEADS):
                lanes = slice(h // 2 * 128, h // 2 * 128 + 128)
                own = h % 2 * 64
                head = slice(h * HEAD_DIM, h * HEAD_DIM + HEAD_DIM)
                mine = low_half if h % 2 == 0 else jnp.logical_not(low_half)
                qa[t, h, own : own + 64, rows] = q[head]
                ka[h, rows, :] = jnp.where(mine, k[:, lanes], kx[rows, :])
                va[t, h, rows, :] = jnp.where(mine, v[:, lanes], ones)
                vt[h, 0:64, rows] = turned[head]
            return 0

        lax.fori_loop(0, count, project, 0)

        def attend(pair, _):
            units = [(parity, *block) for block in blocks_of(length)[0] for parity in range(2)]
            buffers = (score_a, score_b)

            def score(i):
                parity, b, first, store = units[i]
                h, wide = 2 * pair + parity, (b + 1 - first) * BLOCK
                rows = slice(b * BLOCK, b * BLOCK + BLOCK)
                keys = slice(first * BLOCK, b * BLOCK + BLOCK)
                buffers[i % 2][0:wide, :] = mul(ka[h, keys, :], qa[t, h, :, rows])

            def weigh(i):
                parity, b, first, store = units[i]
                h, wide = 2 * pair + parity, (b + 1 - first) * BLOCK
                rows = slice(b * BLOCK, b * BLOCK + BLOCK)
                keys = slice(first * BLOCK, b * BLOCK + BLOCK)
                for half in range(2):
                    low, high = reach(half, b - first, wide)
                    lanes = slice(half * 128, half * 128 + 128)
                    last = edge[1 if b == count - 1 and half == 1 else 0]
                    scores = buffers[i % 2][low : high - 128, lanes]
                    border = buffers[i % 2][high - 128 : high, lanes] + last
                    peak = jnp.max(border, axis=0, keepdims=True)
                    if high - 128 > low:
                        peak = jnp.maximum(peak, jnp.max(scores, axis=0, keepdims=True))
                        expo[t, h, store + low : store + high - 128, lanes] = jnp.exp(scores - peak).astype(bf16)
                    expo[t, h, store + high - 128 : store + high, lanes] = jnp.exp(border - peak).astype(bf16)
                    if low > 0:
                        expo[t, h, store : store + low, lanes] = jnp.zeros((low, 128), bf16)
                    if high < wide:
                        expo[t, h, store + high : store + wide, lanes] = jnp.zeros((wide - high, 128), bf16)
                result = mul(vt[h, :, keys], expo[t, h, store : store + wide, :])
                inv = 1.0 / result[64:72]
                inverse[t, h, :, rows] = inv
                head_rows = pl.ds(pl.multiple_of(h * HEAD_DIM, HEAD_DIM), HEAD_DIM)
                outcome[t, head_rows, rows] = result[0:64] * inv[0:1]

            score(0)
            for i in range(len(units)):
                if i + 1 < len(units):
                    score(i + 1)
                weigh(i)
            return 0

        lax.fori_loop(0, HEADS // 2, attend, 0)

        def feed(b, _):
            rows = rows_at(b)
            turned = outcome[t, :, rows].astype(bf16).T
            middle = xbuf[rows, :] + row_of(ob_ref) + mul(turned, wout_ref[...])
            hat, scale = normalise(middle)
            normed = (hat * row_of(g2_ref) + row_of(b2_ref)).astype(bf16)
            hat2[t, rows, :] = hat
            scales[t, rows, 1:2] = scale
            normed2[t, rows, :] = normed
            total = middle + row_of(db_ref)
            for c in range(wup_ref.shape[1] // 256):
                columns = slice(c * 256, c * 256 + 256)
                hidden = mul(normed, wup_ref[:, columns]) + row_of(ub_ref)[:, columns]
                phi = 0.5 + 0.5 * lax.erf(hidden * 0.7071067811865476)
                density = 0.3989422804014327 * jnp.exp(-0.5 * hidden * hidden)
                act = (hidden * phi).astype(bf16)
                active[t, rows, columns] = act
                slope[t, rows, columns] = (phi + hidden * density).astype(bf16)
                total = total + mul(act, wdown_ref[columns, :])
            state = total.astype(bf16)
            states[t, rows, :] = state
            xbuf[rows, :] = state.astype(f32) + emb_v[rows, :].astype(f32)
            return 0

        lax.fori_loop(0, count, feed, 0)
        return 0

    lax.fori_loop(0, 2, forward, 0)

    for total in (sums, qv_sums, gqkv, gout, gup, gdown):
        total[...] = jnp.zeros_like(total)
    pl.semaphore_wait(barrier, len(peers))
    state_copy().start()
    keep_state = pltpu.make_async_copy(states.at[part], states_hbm.at[part], in_sem.at[0])
    keep_state.start()

    def add_sums(at, values):
        columns = slice(at, at + values.shape[1])
        sums[:, columns] += eight_sums(values)

    def backward(t):
        def feed_back(b, _):
            rows = rows_at(b)
            down = grads[t + 1, rows, :]
            down_wide = down.astype(f32)
            add_sums(DB, down_wide)
            cotangent = jnp.zeros((BLOCK, width), f32)
            for c in range(wup_ref.shape[1] // 256):
                columns = slice(c * 256, c * 256 + 256)
                up = mul_rows(down, wdown_ref[columns, :]) * slope[t, rows, columns].astype(f32)
                up = up.astype(bf16)
                hgrad[rows, columns] = up
                add_sums(UB + c * 256, up.astype(f32))
                cotangent = cotangent + mul_rows(up, wup_ref[:, columns])
            hat = hat2[t, rows, :]
            add_sums(N2G, cotangent * hat)
            add_sums(N2B, cotangent)
            middle = down_wide + norm_back(cotangent, row_of(g2_ref), hat, scales[t, rows, 1:2])
            mgrad[rows, :] = middle
            low = middle.astype(bf16)
            branch[rows, :] = low
            add_sums(OB, low.astype(f32))
            attended_grad = mul_rows(wout_ref[...], low).astype(bf16).astype(f32)
            line = lax.broadcasted_iota(jnp.int32, (16, BLOCK), 0)
            for h in range(HEADS):
                own = h % 2 * 64
                head = slice(h * HEAD_DIM, h * HEAD_DIM + HEAD_DIM)
                scaled = (attended_grad[head] * inverse[t, h, 0:1, rows]).astype(bf16)
                inner = -jnp.sum(scaled.astype(f32) * outcome[t, head, rows], axis=0, keepdims=True)
                high = inner.astype(bf16).astype(f32)
                extra = jnp.where(line == 0, high, jnp.where(line == 1, inner - high, 0.0))
                goa[h, own : own + 64, rows] = scaled
                goa[h, 64 - own : 80 - own, rows] = extra.astype(bf16)
            return 0

        lax.fori_loop(0, count, feed_back, 0)

        gdown[...] += mul_columns(grads[t + 1], active[t])

        if t == 0:
            pack(down, 0, gdown)
            clear(down, DOWN_ROWS)
            sum_down.step()

        gup[...] += mul_columns(normed2[t], hgrad[...])
        gout[...] += mul(outcome[t].astype(bf16), branch[...])

        if t == 0:
            pack(up, 0, gup)
            pack(up, OUT_AT, gout)
            clear(up, UP_ROWS)
            sum_up.step()

        def attend_back(b, first, store):
            rows = slice(b * BLOCK, b * BLOCK + BLOCK)
            keys = slice(first * BLOCK, b * BLOCK + BLOCK)
            wide = (b + 1 - first) * BLOCK
            buffers = (slope_a, slope_b)

            def slopes(h):
                values = mul(va[t, h, keys, :], goa[h, :, rows])
                values = expo[t, h, store : store + wide, :].astype(f32) * values
                buffers[h % 2][0:wide, :] = values.astype(bf16)

            def spread(h):
                head = slice(h * HEAD_DIM, h * HEAD_DIM + HEAD_DIM)
                own = slice(h % 2 * 64, h % 2 * 64 + 64)
                score_grad = buffers[h % 2][0:wide, :]
                query_part = mul(kt[t, head, keys], score_grad)
                pgrad[head, rows] = (query_part * HEAD_DIM**-0.5).astype(bf16)
                key_part = mul_rows(qa[t, h, own, rows], score_grad)
                value_part = mul_rows(goa[h, own, rows], expo[t, h, store : store + wide, :])
                for kb in range(first, b + 1):
                    mine = slice((kb - first) * BLOCK, (kb - first) * BLOCK + BLOCK)
                    there = slice(kb * BLOCK, kb * BLOCK + BLOCK)
                    if b == min(count - 1, kb + SPAN // BLOCK):
                        dkt[head, there] = key_part[:, mine]
                        dvt[head, there] = value_part[:, mine]
                    else:
                        dkt[head, there] += key_part[:, mine]
                        dvt[head, there] += value_part[:, mine]

            slopes(0)
            for h in range(HEADS):
                if h + 1 < HEADS:
                    slopes(h + 1)
                spread(h)

        def input_back(b):
            rows = slice(b * BLOCK, b * BLOCK + BLOCK)
            pgrad[width : 2 * width, rows] = dkt[:, rows].astype(bf16)
            pgrad[2 * width :, rows] = dvt[:, rows].astype(bf16)
            part_grad = pgrad[:, rows]
            for lanes in (slice(0, 128), slice(128, 256)):
                qv_sums[0:width, :] += part_grad[:width, lanes].astype(f32)
                qv_sums[width:, :] += part_grad[2 * width :, lanes].astype(f32)
            cotangent = mul(wqkv_ref[...], part_grad).T
            hat = hat1[t, rows, :]
            add_sums(N1G, cotangent * hat)
            add_sums(N1B, cotangent)
            x_grad = mgrad[rows, :] + norm_back(cotangent, row_of(g1_ref), hat, scales[t, rows, 0:1])
            grads[t, rows, :] = x_grad.astype(bf16)

        def send(now, blocks):
            @pl.when(part == 1 - now)
            def _():
                for b in blocks:
                    main_copy(now, b).start()

            extra = [b for b in blocks if b // (count // 2) == 1 - now]
            if extra:
                @pl.when(part == now)
                def _():
                    for b in extra:
                        extra_copy(now, b).start()

        for b, first, store in reversed(blocks_of(length)[0]):
            attend_back(b, first, store)
            if b + 1 < count:
                input_back(b + 1)
            if t == 0 and b == count - 1:
                sum_down.step()
                sum_up.step()
            if t == 0 and b == count // 2 - 1:
                send(0, range(count // 2, count))

        pgrad[width : 2 * width, 0:BLOCK] = dkt[:, 0:BLOCK].astype(bf16)
        pgrad[2 * width :, 0:BLOCK] = dvt[:, 0:BLOCK].astype(bf16)
        gqkv[...] += mul(pgrad[...], normed1[t])

        if t == 0:
            pack(qkv, 0, gqkv)
            clear(qkv, QKV_ROWS)
            sum_qkv.step()
        input_back(0)
        send(t, range(count // 2 if t == 0 else count))

    backward(1)
    backward(0)

    sums[0:1, QB : QB + width] = jnp.sum(qv_sums[0:width, :].T, axis=0, keepdims=True)
    sums[0:1, VB : VB + width] = jnp.sum(qv_sums[width:, :].T, axis=0, keepdims=True)
    total = jnp.sum(sums[...], axis=0, keepdims=True)
    small[...] = jnp.concatenate([total[:, i * 128 : i * 128 + 128] for i in range(SUMS // 128)], axis=0)
    sum_small.step()
    half_rows = pl.ds(pl.multiple_of(part * (length // 2), BLOCK), length // 2)
    keep_grad = pltpu.make_async_copy(grads.at[part], grads_hbm.at[part], in_sem.at[1])
    keep_extra = pltpu.make_async_copy(grads.at[1 - part, half_rows], extra_hbm.at[part], in_sem.at[2])
    keep_grad.start()
    keep_extra.start()
    for total in (
        sum_qkv, sum_down, sum_up, sum_small,
        sum_down, sum_up, sum_small,
        sum_qkv, sum_down, sum_up, sum_small,
        sum_qkv, sum_down, sum_up, sum_small, sum_qkv, sum_down, sum_up,
    ):
        total.step()

    state_copy().wait()
    for b in range(count):
        main_copy(0, b).wait()
    for b in range(count // 2):
        extra_copy(0, b).wait()
    for keep in (keep_state, keep_grad, keep_extra, sum_small.keep, sum_down.keep, sum_up.keep, sum_qkv.keep):
        keep.wait()


def padded(rows, devices):
    unit = 16 * devices
    return (rows + unit - 1) // unit * unit


def finish_kernel(
    states_hbm, grads_hbm, extra_hbm, down_hbm, up_hbm, qkv_hbm, small_hbm,
    loop_out, grad_out, embed_out, n1g, n1b, gqkv, qb, vb, gout, ob, n2g, n2b, gup, ub, gdown, db,
    states, grads, extra, down, up, qkv, small, grad_v, embed_v, gqkv_v, gout_v, gup_v, gdown_v, sems,
):
    part = lax.axis_index("section")
    length, width = grads.shape[1:]

    def copy(at, src, dst):
        return pltpu.make_async_copy(src, dst, sems.at[at])

    passed = copy(0, states_hbm, states)
    loads = [
        copy(1, grads_hbm, grads), copy(2, extra_hbm, extra), copy(3, up_hbm, up), copy(4, down_hbm, down),
        copy(12, qkv_hbm, qkv), copy(13, small_hbm, small),
    ]
    passed.start()
    for load in loads:
        load.start()
    passed.wait()
    stores = [copy(11, states, loop_out.at[0])]
    stores[-1].start()
    loads[0].wait()
    grad_v[...] = grads[...].astype(f32)
    stores.append(copy(5, grad_v, grad_out.at[0]))
    stores[-1].start()
    loads[1].wait()
    half_rows = pl.ds(pl.multiple_of(part * (length // 2), BLOCK), length // 2)
    embed_v[...] = grads[:, half_rows, :].astype(f32) + extra[...].astype(f32)
    stores.append(copy(6, embed_v, embed_out))
    stores[-1].start()
    loads[2].wait()
    for i in range(gup_v.shape[1] // 128):
        lanes = slice(i * 128, i * 128 + 128)
        gup_v[:, lanes] = up[i * width : (i + 1) * width, :].astype(f32)
    stores.append(copy(7, gup_v, gup))
    stores[-1].start()
    for i in range(width // 128):
        at = OUT_AT + i * width
        gout_v[:, i * 128 : i * 128 + 128] = up[at : at + width, :].astype(f32)
    stores.append(copy(9, gout_v, gout))
    stores[-1].start()
    loads[3].wait()
    for i in range(gup_v.shape[1] // 128):
        gdown_v[i * 128 : i * 128 + 128, :] = down[i * width : (i + 1) * width, :].T.astype(f32)
    stores.append(copy(8, gdown_v, gdown))
    stores[-1].start()
    loads[4].wait()
    for i in range(width // 128):
        turned = qkv[i * 3 * width : (i + 1) * 3 * width, :].T
        gqkv_v[i * 128 : i * 128 + 128, :] = turned.astype(f32)
    stores.append(copy(10, gqkv_v, gqkv))
    stores[-1].start()
    loads[5].wait()
    for at, ref in ((N1G, n1g), (N1B, n1b), (QB, qb), (VB, vb), (OB, ob), (N2G, n2g), (N2B, n2b), (DB, db), (UB, ub)):
        for i in range(ref.shape[0] // 128):
            ref[i * 128 : i * 128 + 128] = small[at // 128 + i]
    for store in stores:
        store.wait()


def whole_block(sections, places, *args):
    start = args[0]
    _, length, width = start.shape
    hidden = args[15].shape[0]
    vmem = pl.BlockSpec(memory_space=pltpu.VMEM)
    smem = pl.BlockSpec(memory_space=pltpu.SMEM)
    hbm = pl.BlockSpec(memory_space=pl.ANY)
    count = length // BLOCK
    devices = sections * places
    far_count = places // 4
    payloads = [padded(rows, devices) for rows in (DOWN_ROWS, UP_ROWS, QKV_ROWS)]

    def V(*shape, dtype=bf16):
        return pltpu.VMEM(shape, dtype)

    def O(*shape, dtype=f32):
        return jax.ShapeDtypeStruct(shape, dtype)

    def sum_buffers(rows):
        return [
            V(rows, 128),
            V(rows // 2, 128),
            V(3, rows // 8, 128),
            V(far_count - 1, rows // devices, 128),
            V(rows, 128),
        ]

    copies = 2 * (6 + 2 * far_count) + devices + 2 + far_count
    between = pl.pallas_call(
        partial(compute_kernel, far_count),
        name="block_both_ways",
        in_specs=[hbm, hbm, hbm, vmem, smem] + [vmem] * 13,
        out_specs=[hbm] * 7,
        out_shape=[
            O(2, length, width, dtype=bf16),
            O(2, length, width, dtype=bf16),
            O(2, length // 2, width, dtype=bf16),
            *(O(rows, 128, dtype=bf16) for rows in payloads),
            O(SUMS // 128, 128),
        ],
        scratch_shapes=[
            V(length, width),
            V(length, width),
            V(length, 128),
            V(width, width),
            V(width, 128, dtype=f32),
            V(2, 128, 128, dtype=f32),
            V(SPAN + BLOCK, BLOCK, dtype=f32),
            V(SPAN + BLOCK, BLOCK, dtype=f32),
            V(SPAN + BLOCK, BLOCK),
            V(SPAN + BLOCK, BLOCK),
            V(length, width, dtype=f32),
            V(2, length, width, dtype=f32),
            V(2, length, 128, dtype=f32),
            V(2, length, width),
            V(2, HEADS, 128, length),
            V(HEADS, length, 128),
            V(2, width, length),
            V(2, HEADS, length, 128),
            V(HEADS, 80, length),
            V(2, HEADS, blocks_of(length)[1], BLOCK),
            V(2, HEADS, 8, length, dtype=f32),
            V(2, width, length, dtype=f32),
            V(2, length, width, dtype=f32),
            V(2, length, width),
            V(2, length, hidden),
            V(2, length, hidden),
            V(length, hidden),
            V(length, width),
            V(length, width, dtype=f32),
            V(3, length, width),
            V(2, length, width),
            V(HEADS, 128, length),
            V(width, length, dtype=f32),
            V(width, length, dtype=f32),
            V(3 * width, length),
            V(3 * width, width, dtype=f32),
            V(width, width, dtype=f32),
            V(width, hidden, dtype=f32),
            V(width, hidden, dtype=f32),
            V(8, SUMS, dtype=f32),
            V(2 * width, 128, dtype=f32),
        ]
        + sum_buffers(payloads[0])
        + sum_buffers(payloads[1])
        + [
            V(payloads[2], 128),
            V(payloads[2] // 2, 128),
            V(devices // 2 - 1, payloads[2] // devices, 128),
            V(payloads[2], 128),
        ]
        + [
            V(SUMS // 128, 128, dtype=f32),
            V(2 + far_count, SUMS // 128, 128, dtype=f32),
            pltpu.SemaphoreType.DMA((7,)),
            pltpu.SemaphoreType.DMA((1 + count + count // 2,)),
            pltpu.SemaphoreType.DMA((1 + count + count // 2,)),
            pltpu.SemaphoreType.DMA((copies,)),
            pltpu.SemaphoreType.DMA((copies,)),
        ],
        compiler_params=pltpu.CompilerParams(
            vmem_limit_bytes=63 << 20, collective_id=0, has_side_effects=True
        ),
    )(*args)
    return pl.pallas_call(
        finish_kernel,
        name="widen",
        in_specs=[hbm] * 7,
        out_specs=[hbm, hbm, hbm, vmem, vmem, hbm, vmem, vmem, hbm, vmem, vmem, vmem, hbm, vmem, hbm, vmem],
        out_shape=[
            O(1, 2, length, width, dtype=bf16),
            O(1, 2, length, width),
            O(2, length // 2, width),
            O(width), O(width), O(width, 3 * width), O(width), O(width), O(width, width), O(width),
            O(width), O(width), O(width, hidden), O(hidden), O(hidden, width), O(width),
        ],
        scratch_shapes=[
            V(2, length, width),
            V(2, length, width),
            V(2, length // 2, width),
            V(payloads[0], 128),
            V(payloads[1], 128),
            V(payloads[2], 128),
            V(SUMS // 128, 128, dtype=f32),
            V(2, length, width, dtype=f32),
            V(2, length // 2, width, dtype=f32),
            V(width, 3 * width, dtype=f32),
            V(width, width, dtype=f32),
            V(width, hidden, dtype=f32),
            V(hidden, width, dtype=f32),
            pltpu.SemaphoreType.DMA((14,)),
        ],
        compiler_params=pltpu.CompilerParams(vmem_limit_bytes=63 << 20),
    )(*between)


def solution(mesh):
    rows = P("dp", None, None)
    return jax.shard_map(
        partial(whole_block, mesh.shape["section"], mesh.shape["dp"]),
        mesh=mesh,
        in_specs=(rows, rows, rows, P("dp", None), P("dp")) + (P(),) * 13,
        out_specs=(
            P("section", "dp", None, None),
            P("section", "dp", None, None),
            P("dp", "section", None),
        )
        + (P(),) * 13,
        check_vma=False,
    )
```

time: 101 us -> 85.4 us (0.85)
  Pallas kernels: 94 us -> 84.3 us
  local copies, waits for them, and re-layouts: 5.79 us -> 0 us
    pallas_call x1, Pallas kernels: 90.1 us -> 79.3 us  [whole_block(): pl.pallas_call(partial(compute_kernel, far_count), name='block_both_ways'...]
    unnamed x10 -> x0, local copies, waits for them, and re-layouts: 5.79 us -> none
    pallas_call x1, Pallas kernels: 3.87 us -> 5.05 us  [whole_block(): pl.pallas_call(finish_kernel, name='widen', in_specs=[hbm] * 7, out_specs...]
where the time goes in v3:
time: 85.4 us; the launch traced here: 85.2 us
  Pallas kernels  84.3 us (99%)
    pallas_call x1, Pallas kernels, whole_block(): pl.pallas_call(partial(compute_kernel, far_count), name='block_both_ways'...  79.3 us
    pallas_call x1, Pallas kernels, whole_block(): pl.pallas_call(finish_kernel, name='widen', in_specs=[hbm] * 7, out_specs...  5.05 us

profile of v3, /device:TPU:0, one launch (start us, length us, event | category | flops | bytes accessed | tf_op | source)
XLA Modules:
  0.0 85.2 jit_solution(8654756493850189899)
XLA Ops:
  0.7 79.3 %block_both_ways.1 = (bf16[2,1024,256]{2,1,0:T(8,128)(2,1)}, bf16[2,1024,256]{2,1,0:T(8,128)(2,1)}, bf16[2,512,256]{2,1,0:T(8,128)(2,1)}, bf16[2048,128]{1,0:T(8...) custom-call(bf16[2,1024,256]{2,1,0:T(8,128)(2,1)} %start_hbm.1, ...), custom_call_target="tpu_custom_call" | custom-call | tf_op jit(solution)/shard_map/block_both_ways/pallas_call | solution.py:743
  80.0 5.0 %widen.1 = (bf16[1,2,1024,256]{3,2,1,0:T(8,128)(2,1)}, f32[1,2,1024,256]{3,2,1,0:T(8,128)}, f32[2,512,256]{2,1,0:T(8,128)}, f32[256]{0:T(256)}, f32[256]{0:T(256...) custom-call(bf16[2,1024,256]{2,1,0:T(8,128)(2,1)} %get-tuple-element, ...), custom_call_target="tpu_custom_call" | custom-call | tf_op jit(solution)/shard_map/widen/pallas_call | solution.py:819

commit v4 on v3

--- a/solution.py
+++ b/solution.py
@@ -79,7 +79,7 @@
     g1_ref, b1_ref, wqkv_ref, qb_ref, vb_ref, wout_ref, ob_ref, g2_ref, b2_ref, wup_ref, ub_ref,
     wdown_ref, db_ref,
     states_hbm, grads_hbm, extra_hbm, down_hbm, up_hbm, qkv_hbm, small_hbm,
-    start_v, emb_v, kx, wq_t, qb_t, edge, score_a, score_b, slope_a, slope_b,
+    start_v, emb_v, kx, wq_t, qb_t, edge, score_a, score_b, score_c, score_d, slope_a, slope_b,
     xbuf, hat1, scales, normed1, qa, ka, kt, va, vt, expo, inverse,
     outcome, hat2, normed2, active, slope, hgrad, branch, mgrad, grads, states, goa,
     dkt, dvt, pgrad, gqkv, gout, gup, gdown, sums, qv_sums,
@@ -391,18 +391,18 @@
                 vt[h, 0:64, rows] = turned[head]
             return 0
 
-        lax.fori_loop(0, count, project, 0)
+        lax.fori_loop(0, count, project, 0, unroll=4)
 
         def attend(pair, _):
             units = [(parity, *block) for block in blocks_of(length)[0] for parity in range(2)]
-            buffers = (score_a, score_b)
+            buffers = (score_a, score_b, score_c, score_d)
 
             def score(i):
                 parity, b, first, store = units[i]
                 h, wide = 2 * pair + parity, (b + 1 - first) * BLOCK
                 rows = slice(b * BLOCK, b * BLOCK + BLOCK)
                 keys = slice(first * BLOCK, b * BLOCK + BLOCK)
-                buffers[i % 2][0:wide, :] = mul(ka[h, keys, :], qa[t, h, :, rows])
+                buffers[i % 4][0:wide, :] = mul(ka[h, keys, :], qa[t, h, :, rows])
 
             def weigh(i):
                 parity, b, first, store = units[i]
@@ -413,8 +413,8 @@
                     low, high = reach(half, b - first, wide)
                     lanes = slice(half * 128, half * 128 + 128)
                     last = edge[1 if b == count - 1 and half == 1 else 0]
-                    scores = buffers[i % 2][low : high - 128, lanes]
-                    border = buffers[i % 2][high - 128 : high, lanes] + last
+                    scores = buffers[i % 4][low : high - 128, lanes]
+                    border = buffers[i % 4][high - 128 : high, lanes] + last
                     peak = jnp.max(border, axis=0, keepdims=True)
                     if high - 128 > low:
                         peak = jnp.maximum(peak, jnp.max(scores, axis=0, keepdims=True))
@@ -431,13 +431,16 @@
                 outcome[t, head_rows, rows] = result[0:64] * inv[0:1]
 
             score(0)
-            for i in range(len(units)):
-                if i + 1 < len(units):
-                    score(i + 1)
+            score(1)
+            for i in range(0, len(units), 2):
+                if i + 2 < len(units):
+                    score(i + 2)
+                    score(i + 3)
                 weigh(i)
+                weigh(i + 1)
             return 0
 
-        lax.fori_loop(0, HEADS // 2, attend, 0)
+        lax.fori_loop(0, HEADS // 2, attend, 0, unroll=2)
 
         def feed(b, _):
             rows = rows_at(b)
@@ -448,22 +451,21 @@
             hat2[t, rows, :] = hat
             scales[t, rows, 1:2] = scale
             normed2[t, rows, :] = normed
-            total = middle + row_of(db_ref)
             for c in range(wup_ref.shape[1] // 256):
                 columns = slice(c * 256, c * 256 + 256)
                 hidden = mul(normed, wup_ref[:, columns]) + row_of(ub_ref)[:, columns]
-                phi = 0.5 + 0.5 * lax.erf(hidden * 0.7071067811865476)
-                density = 0.3989422804014327 * jnp.exp(-0.5 * hidden * hidden)
-                act = (hidden * phi).astype(bf16)
-                active[t, rows, columns] = act
-                slope[t, rows, columns] = (phi + hidden * density).astype(bf16)
-                total = total + mul(act, wdown_ref[columns, :])
+                inner = hidden * 0.7071067811865476
+                phi = 0.5 * lax.erf(inner) + 0.5
+                bell = jnp.exp2(inner * -1.4426950408889634 * inner)
+                active[t, rows, columns] = (hidden * phi).astype(bf16)
+                slope[t, rows, columns] = (phi + hidden * bell * 0.3989422804014327).astype(bf16)
+            total = middle + row_of(db_ref) + mul(active[t, rows, :], wdown_ref[...])
             state = total.astype(bf16)
             states[t, rows, :] = state
             xbuf[rows, :] = state.astype(f32) + emb_v[rows, :].astype(f32)
             return 0
 
-        lax.fori_loop(0, count, feed, 0)
+        lax.fori_loop(0, count, feed, 0, unroll=4)
         return 0
 
     lax.fori_loop(0, 2, forward, 0)
@@ -485,14 +487,13 @@
             down = grads[t + 1, rows, :]
             down_wide = down.astype(f32)
             add_sums(DB, down_wide)
-            cotangent = jnp.zeros((BLOCK, width), f32)
             for c in range(wup_ref.shape[1] // 256):
                 columns = slice(c * 256, c * 256 + 256)
-                up = mul_rows(down, wdown_ref[columns, :]) * slope[t, rows, columns].astype(f32)
-                up = up.astype(bf16)
-                hgrad[rows, columns] = up
-                add_sums(UB + c * 256, up.astype(f32))
-                cotangent = cotangent + mul_rows(up, wup_ref[:, columns])
+                up_grad = mul_rows(down, wdown_ref[columns, :]) * slope[t, rows, columns].astype(f32)
+                up_grad = up_grad.astype(bf16)
+                hgrad[rows, columns] = up_grad
+                add_sums(UB + c * 256, up_grad.astype(f32))
+            cotangent = mul_rows(hgrad[rows, :], wup_ref[...])
             hat = hat2[t, rows, :]
             add_sums(N2G, cotangent * hat)
             add_sums(N2B, cotangent)
@@ -514,7 +515,7 @@
                 goa[h, 64 - own : 80 - own, rows] = extra.astype(bf16)
             return 0
 
-        lax.fori_loop(0, count, feed_back, 0)
+        lax.fori_loop(0, count, feed_back, 0, unroll=4)
 
         gdown[...] += mul_columns(grads[t + 1], active[t])
 
@@ -759,6 +760,8 @@
             V(width, width),
             V(width, 128, dtype=f32),
             V(2, 128, 128, dtype=f32),
+            V(SPAN + BLOCK, BLOCK, dtype=f32),
+            V(SPAN + BLOCK, BLOCK, dtype=f32),
             V(SPAN + BLOCK, BLOCK, dtype=f32),
             V(SPAN + BLOCK, BLOCK, dtype=f32),
             V(SPAN + BLOCK, BLOCK),

time: 85.4 us -> 78 us (0.913)
  Pallas kernels: 84.3 us -> 76.9 us
    pallas_call x1, Pallas kernels: 79.3 us -> 71.9 us  [whole_block(): pl.pallas_call(partial(compute_kernel, far_count), name='block_both_ways'...]
where the time goes in v4:
time: 78 us; the launch traced here: 77.8 us
  Pallas kernels  76.9 us (99%)
  between operations  0.84 us (1%)
    pallas_call x1, Pallas kernels, whole_block(): pl.pallas_call(partial(compute_kernel, far_count), name='block_both_ways'...  71.9 us
    pallas_call x1, Pallas kernels, whole_block(): pl.pallas_call(finish_kernel, name='widen', in_specs=[hbm] * 7, out_specs...  5.05 us

profile of v4, /device:TPU:0, one launch (start us, length us, event | category | flops | bytes accessed | tf_op | source)
XLA Modules:
  0.0 77.8 jit_solution(2566992999259571512)
XLA Ops:
  0.7 71.9 %block_both_ways.1 = (bf16[2,1024,256]{2,1,0:T(8,128)(2,1)}, bf16[2,1024,256]{2,1,0:T(8,128)(2,1)}, bf16[2,512,256]{2,1,0:T(8,128)(2,1)}, bf16[2048,128]{1,0:T(8...) custom-call(bf16[2,1024,256]{2,1,0:T(8,128)(2,1)} %start_hbm.1, ...), custom_call_target="tpu_custom_call" | custom-call | tf_op jit(solution)/shard_map/block_both_ways/pallas_call | solution.py:744
  72.5 5.0 %widen.1 = (bf16[1,2,1024,256]{3,2,1,0:T(8,128)(2,1)}, f32[1,2,1024,256]{3,2,1,0:T(8,128)}, f32[2,512,256]{2,1,0:T(8,128)}, f32[256]{0:T(256)}, f32[256]{0:T(256...) custom-call(bf16[2,1024,256]{2,1,0:T(8,128)(2,1)} %get-tuple-element, ...), custom_call_target="tpu_custom_call" | custom-call | tf_op jit(solution)/shard_map/widen/pallas_call | solution.py:822

commit v5 on v4

--- a/solution.py
+++ b/solution.py
@@ -67,6 +67,7 @@
     return low, wide - (128 if half == 0 else 0)
 
 
+HOOKS = {"a3": "DU", "f2": "Q32", "f0": "10"}
 N1G, N1B, QB, VB, OB, N2G, N2B, DB, UB = (256 * i for i in range(9))
 SUMS = 256 * 12
 DOWN_ROWS, OUT_AT, UP_ROWS, QKV_ROWS = 2048, 2048, 2560, 1536
@@ -136,7 +137,9 @@
             plane_at = core_at + plane * quarter
             self.sizes = (half, quarter, piece)
             self.starts = (core_at, plane_at, plane_at + far * piece)
-            self.keep = pltpu.make_async_copy(result, result_hbm, in_sem.at[4 + (first_sem > 0)])
+            self.result_hbm = result_hbm
+            rows = self.rows(core_at, half)
+            self.keep = pltpu.make_async_copy(result.at[rows], result_hbm.at[rows], in_sem.at[4 + (first_sem > 0)])
             self.stage = 0
 
         def rows(self, at, size):
@@ -168,7 +171,8 @@
                 return [self.copy(first + step, src, src, far_peer(step)) for step in range(1, far_count)]
             if level == 1:
                 return [self.copy(first + far_count - 1 + step, src, src, plane_peer(step)) for step in range(1, 4)]
-            return [self.copy(first + far_count + 3, src, src, core_peer)]
+            rows = self.rows(self.starts[0], self.sizes[0])
+            return [self.copy(first + far_count + 3, src, self.result_hbm.at[rows], core_peer)]
 
         def add(self, level):
             rows = self.rows(self.starts[level], self.sizes[level])
@@ -194,7 +198,7 @@
                 start(self.out(stage))
             elif stage <= 5:
                 start(self.back(5 - stage))
-            else:
+            if stage == 5:
                 self.keep.start()
 
     class ShortSum:
@@ -205,7 +209,9 @@
             self.piece = self.half // chips
             self.core_at = core * self.half
             self.chip_at = self.core_at + chip * self.piece
-            self.keep = pltpu.make_async_copy(result, result_hbm, in_sem.at[6])
+            self.result_hbm = result_hbm
+            rows = self.rows(self.core_at, self.half)
+            self.keep = pltpu.make_async_copy(result.at[rows], result_hbm.at[rows], in_sem.at[6])
             self.stage = 0
 
         def rows(self, at, size):
@@ -230,8 +236,8 @@
             return [self.copy(chips - 1 + step, src, src, chip_peer(step)) for step in range(1, chips)]
 
         def core_back(self):
-            src = self.result.at[self.rows(self.core_at, self.half)]
-            return [self.copy(2 * chips - 1, src, src, core_peer)]
+            rows = self.rows(self.core_at, self.half)
+            return [self.copy(2 * chips - 1, self.result.at[rows], self.result_hbm.at[rows], core_peer)]
 
         def step(self):
             stage = self.stage
@@ -255,9 +261,9 @@
             elif stage == 3:
                 finish(self.chip_back())
                 start(self.core_back())
+                self.keep.start()
             else:
                 finish(self.core_back())
-                self.keep.start()
 
     class Small:
         def __init__(self, first_sem):
@@ -366,7 +372,7 @@
     def rows_at(b):
         return pl.ds(pl.multiple_of(b * BLOCK, BLOCK), BLOCK)
 
-    def forward(t, _):
+    def forward(t):
         def project(b, _):
             rows = rows_at(b)
             hat, scale = normalise(xbuf[rows, :])
@@ -466,22 +472,53 @@
             return 0
 
         lax.fori_loop(0, count, feed, 0, unroll=4)
-        return 0
-
-    lax.fori_loop(0, 2, forward, 0)
-
-    for total in (sums, qv_sums, gqkv, gout, gup, gdown):
+    forward(0)
+    forward(1)
+
+    for total in (sums, qv_sums):
         total[...] = jnp.zeros_like(total)
     pl.semaphore_wait(barrier, len(peers))
     state_copy().start()
     keep_state = pltpu.make_async_copy(states.at[part], states_hbm.at[part], in_sem.at[0])
     keep_state.start()
 
+    def add_to(total, term, t):
+        if t == 1:
+            total[...] = term
+        else:
+            total[...] += term
+
     def add_sums(at, values):
         columns = slice(at, at + values.shape[1])
         sums[:, columns] += eight_sums(values)
 
+    def send(now, blocks):
+        @pl.when(part == 1 - now)
+        def _():
+            for b in blocks:
+                main_copy(now, b).start()
+
+        extra = [b for b in blocks if b // (count // 2) == 1 - now]
+        if extra:
+            @pl.when(part == now)
+            def _():
+                for b in extra:
+                    extra_copy(now, b).start()
+
+    totals = {"D": sum_down, "U": sum_up, "Q": sum_qkv, "S": sum_small}
+
+    def perform(action):
+        if action in totals:
+            totals[action].step()
+        else:
+            send(0, [int(action)])
+
     def backward(t):
+        def hook(point):
+            if t == 0:
+                for action in HOOKS.get(point, ()):
+                    perform(action)
+
         def feed_back(b, _):
             rows = rows_at(b)
             down = grads[t + 1, rows, :]
@@ -517,15 +554,14 @@
 
         lax.fori_loop(0, count, feed_back, 0, unroll=4)
 
-        gdown[...] += mul_columns(grads[t + 1], active[t])
-
+        add_to(gdown, mul_columns(grads[t + 1], active[t]), t)
         if t == 0:
             pack(down, 0, gdown)
             clear(down, DOWN_ROWS)
             sum_down.step()
 
-        gup[...] += mul_columns(normed2[t], hgrad[...])
-        gout[...] += mul(outcome[t].astype(bf16), branch[...])
+        add_to(gup, mul_columns(normed2[t], hgrad[...]), t)
+        add_to(gout, mul(outcome[t].astype(bf16), branch[...]), t)
 
         if t == 0:
             pack(up, 0, gup)
@@ -570,8 +606,9 @@
 
         def input_back(b):
             rows = slice(b * BLOCK, b * BLOCK + BLOCK)
-            pgrad[width : 2 * width, rows] = dkt[:, rows].astype(bf16)
-            pgrad[2 * width :, rows] = dvt[:, rows].astype(bf16)
+            if t == 1:
+                pgrad[width : 2 * width, rows] = dkt[:, rows].astype(bf16)
+                pgrad[2 * width :, rows] = dvt[:, rows].astype(bf16)
             part_grad = pgrad[:, rows]
             for lanes in (slice(0, 128), slice(128, 256)):
                 qv_sums[0:width, :] += part_grad[:width, lanes].astype(f32)
@@ -583,39 +620,32 @@
             x_grad = mgrad[rows, :] + norm_back(cotangent, row_of(g1_ref), hat, scales[t, rows, 0:1])
             grads[t, rows, :] = x_grad.astype(bf16)
 
-        def send(now, blocks):
-            @pl.when(part == 1 - now)
-            def _():
-                for b in blocks:
-                    main_copy(now, b).start()
-
-            extra = [b for b in blocks if b // (count // 2) == 1 - now]
-            if extra:
-                @pl.when(part == now)
-                def _():
-                    for b in extra:
-                        extra_copy(now, b).start()
-
+        last = t == 0
         for b, first, store in reversed(blocks_of(length)[0]):
             attend_back(b, first, store)
-            if b + 1 < count:
+            if b + 1 < count and (False or not last):
                 input_back(b + 1)
-            if t == 0 and b == count - 1:
-                sum_down.step()
-                sum_up.step()
-            if t == 0 and b == count // 2 - 1:
-                send(0, range(count // 2, count))
-
+                if not last and True:
+                    send(1, [b + 1])
+            hook(f"a{b}")
         pgrad[width : 2 * width, 0:BLOCK] = dkt[:, 0:BLOCK].astype(bf16)
         pgrad[2 * width :, 0:BLOCK] = dvt[:, 0:BLOCK].astype(bf16)
-        gqkv[...] += mul(pgrad[...], normed1[t])
-
-        if t == 0:
+        if last and not False:
+            for b in range(1, count):
+                rows = slice(b * BLOCK, b * BLOCK + BLOCK)
+                pgrad[width : 2 * width, rows] = dkt[:, rows].astype(bf16)
+                pgrad[2 * width :, rows] = dvt[:, rows].astype(bf16)
+        add_to(gqkv, mul(pgrad[...], normed1[t]), t)
+        if last:
             pack(qkv, 0, gqkv)
             clear(qkv, QKV_ROWS)
             sum_qkv.step()
-        input_back(0)
-        send(t, range(count // 2 if t == 0 else count))
+            hook("q")
+        for b in reversed(range(1 if False or not last else count)):
+            input_back(b)
+            hook(f"f{b}")
+        if not last:
+            send(1, [0] if True else range(count))
 
     backward(1)
     backward(0)
@@ -630,13 +660,8 @@
     keep_extra = pltpu.make_async_copy(grads.at[1 - part, half_rows], extra_hbm.at[part], in_sem.at[2])
     keep_grad.start()
     keep_extra.start()
-    for total in (
-        sum_qkv, sum_down, sum_up, sum_small,
-        sum_down, sum_up, sum_small,
-        sum_qkv, sum_down, sum_up, sum_small,
-        sum_qkv, sum_down, sum_up, sum_small, sum_qkv, sum_down, sum_up,
-    ):
-        total.step()
+    for action in "DUSDUSQDUSQDUSQDU":
+        perform(action)
 
     state_copy().wait()
     for b in range(count):

time: 78 us -> 75.6 us (0.969)
  Pallas kernels: 76.9 us -> 74.6 us
    pallas_call x1, Pallas kernels: 71.9 us -> 69.6 us  [whole_block(): pl.pallas_call(partial(compute_kernel, far_count), name='block_both_ways'...]
where the time goes in v5:
time: 75.6 us; the launch traced here: 75.4 us
  Pallas kernels  74.6 us (99%)
  between operations  0.84 us (1%)
    pallas_call x1, Pallas kernels, whole_block(): pl.pallas_call(partial(compute_kernel, far_count), name='block_both_ways'...  69.6 us
    pallas_call x1, Pallas kernels, whole_block(): pl.pallas_call(finish_kernel, name='widen', in_specs=[hbm] * 7, out_specs...  5.05 us

profile of v5, /device:TPU:0, one launch (start us, length us, event | category | flops | bytes accessed | tf_op | source)
XLA Modules:
  0.0 75.4 jit_solution(4699598948686366491)
XLA Ops:
  0.7 69.6 %block_both_ways.1 = (bf16[2,1024,256]{2,1,0:T(8,128)(2,1)}, bf16[2,1024,256]{2,1,0:T(8,128)(2,1)}, bf16[2,512,256]{2,1,0:T(8,128)(2,1)}, bf16[2048,128]{1,0:T(8...) custom-call(bf16[2,1024,256]{2,1,0:T(8,128)(2,1)} %start_hbm.1, ...), custom_call_target="tpu_custom_call" | custom-call | tf_op jit(solution)/shard_map/block_both_ways/pallas_call | solution.py:769
  70.2 5.0 %widen.1 = (bf16[1,2,1024,256]{3,2,1,0:T(8,128)(2,1)}, f32[1,2,1024,256]{3,2,1,0:T(8,128)}, f32[2,512,256]{2,1,0:T(8,128)}, f32[256]{0:T(256)}, f32[256]{0:T(256...) custom-call(bf16[2,1024,256]{2,1,0:T(8,128)(2,1)} %get-tuple-element, ...), custom_call_target="tpu_custom_call" | custom-call | tf_op jit(solution)/shard_map/widen/pallas_call | solution.py:847

commit v6 on v5

--- a/solution.py
+++ b/solution.py
@@ -67,7 +67,7 @@
     return low, wide - (128 if half == 0 else 0)
 
 
-HOOKS = {"a3": "DU", "f2": "Q32", "f0": "10"}
+HOOKS = {"a3": "DU", "f2": "Q32", "f1": "D", "f0": "U10"}
 N1G, N1B, QB, VB, OB, N2G, N2B, DB, UB = (256 * i for i in range(9))
 SUMS = 256 * 12
 DOWN_ROWS, OUT_AT, UP_ROWS, QKV_ROWS = 2048, 2048, 2560, 1536
@@ -80,7 +80,7 @@
     g1_ref, b1_ref, wqkv_ref, qb_ref, vb_ref, wout_ref, ob_ref, g2_ref, b2_ref, wup_ref, ub_ref,
     wdown_ref, db_ref,
     states_hbm, grads_hbm, extra_hbm, down_hbm, up_hbm, qkv_hbm, small_hbm,
-    start_v, emb_v, kx, wq_t, qb_t, edge, score_a, score_b, score_c, score_d, slope_a, slope_b,
+    start_v, emb_v, kx, wq_t, qb_t, edge, score_a, score_b, score_c, score_d, slope_a, slope_b, slope_c, slope_d,
     xbuf, hat1, scales, normed1, qa, ka, kt, va, vt, expo, inverse,
     outcome, hat2, normed2, active, slope, hgrad, branch, mgrad, grads, states, goa,
     dkt, dvt, pgrad, gqkv, gout, gup, gdown, sums, qv_sums,
@@ -527,9 +527,8 @@
             for c in range(wup_ref.shape[1] // 256):
                 columns = slice(c * 256, c * 256 + 256)
                 up_grad = mul_rows(down, wdown_ref[columns, :]) * slope[t, rows, columns].astype(f32)
-                up_grad = up_grad.astype(bf16)
-                hgrad[rows, columns] = up_grad
-                add_sums(UB + c * 256, up_grad.astype(f32))
+                hgrad[rows, columns] = up_grad.astype(bf16)
+                add_sums(UB + c * 256, up_grad)
             cotangent = mul_rows(hgrad[rows, :], wup_ref[...])
             hat = hat2[t, rows, :]
             add_sums(N2G, cotangent * hat)
@@ -538,7 +537,7 @@
             mgrad[rows, :] = middle
             low = middle.astype(bf16)
             branch[rows, :] = low
-            add_sums(OB, low.astype(f32))
+            add_sums(OB, middle)
             attended_grad = mul_rows(wout_ref[...], low).astype(bf16).astype(f32)
             line = lax.broadcasted_iota(jnp.int32, (16, BLOCK), 0)
             for h in range(HEADS):
@@ -569,40 +568,38 @@
             clear(up, UP_ROWS)
             sum_up.step()
 
-        def attend_back(b, first, store):
+        buffers = (slope_a, slope_b, slope_c, slope_d)
+
+        def slopes(i):
+            b, first, store, h = units[i]
             rows = slice(b * BLOCK, b * BLOCK + BLOCK)
             keys = slice(first * BLOCK, b * BLOCK + BLOCK)
             wide = (b + 1 - first) * BLOCK
-            buffers = (slope_a, slope_b)
-
-            def slopes(h):
-                values = mul(va[t, h, keys, :], goa[h, :, rows])
-                values = expo[t, h, store : store + wide, :].astype(f32) * values
-                buffers[h % 2][0:wide, :] = values.astype(bf16)
-
-            def spread(h):
-                head = slice(h * HEAD_DIM, h * HEAD_DIM + HEAD_DIM)
-                own = slice(h % 2 * 64, h % 2 * 64 + 64)
-                score_grad = buffers[h % 2][0:wide, :]
-                query_part = mul(kt[t, head, keys], score_grad)
-                pgrad[head, rows] = (query_part * HEAD_DIM**-0.5).astype(bf16)
-                key_part = mul_rows(qa[t, h, own, rows], score_grad)
-                value_part = mul_rows(goa[h, own, rows], expo[t, h, store : store + wide, :])
-                for kb in range(first, b + 1):
-                    mine = slice((kb - first) * BLOCK, (kb - first) * BLOCK + BLOCK)
-                    there = slice(kb * BLOCK, kb * BLOCK + BLOCK)
-                    if b == min(count - 1, kb + SPAN // BLOCK):
-                        dkt[head, there] = key_part[:, mine]
-                        dvt[head, there] = value_part[:, mine]
-                    else:
-                        dkt[head, there] += key_part[:, mine]
-                        dvt[head, there] += value_part[:, mine]
-
-            slopes(0)
-            for h in range(HEADS):
-                if h + 1 < HEADS:
-                    slopes(h + 1)
-                spread(h)
+            values = mul(va[t, h, keys, :], goa[h, :, rows])
+            values = expo[t, h, store : store + wide, :].astype(f32) * values
+            buffers[i % 4][0:wide, :] = values.astype(bf16)
+
+        def spread(i):
+            b, first, store, h = units[i]
+            rows = slice(b * BLOCK, b * BLOCK + BLOCK)
+            keys = slice(first * BLOCK, b * BLOCK + BLOCK)
+            wide = (b + 1 - first) * BLOCK
+            head = slice(h * HEAD_DIM, h * HEAD_DIM + HEAD_DIM)
+            own = slice(h % 2 * 64, h % 2 * 64 + 64)
+            score_grad = buffers[i % 4][0:wide, :]
+            query_part = mul(kt[t, head, keys], score_grad)
+            pgrad[head, rows] = (query_part * HEAD_DIM**-0.5).astype(bf16)
+            key_part = mul_rows(qa[t, h, own, rows], score_grad)
+            value_part = mul_rows(goa[h, own, rows], expo[t, h, store : store + wide, :])
+            for kb in range(first, b + 1):
+                mine = slice((kb - first) * BLOCK, (kb - first) * BLOCK + BLOCK)
+                there = slice(kb * BLOCK, kb * BLOCK + BLOCK)
+                if b == min(count - 1, kb + SPAN // BLOCK):
+                    dkt[head, there] = key_part[:, mine]
+                    dvt[head, there] = value_part[:, mine]
+                else:
+                    dkt[head, there] += key_part[:, mine]
+                    dvt[head, there] += value_part[:, mine]
 
         def input_back(b):
             rows = slice(b * BLOCK, b * BLOCK + BLOCK)
@@ -621,8 +618,18 @@
             grads[t, rows, :] = x_grad.astype(bf16)
 
         last = t == 0
-        for b, first, store in reversed(blocks_of(length)[0]):
-            attend_back(b, first, store)
+        units = [(*block, h) for block in reversed(blocks_of(length)[0]) for h in range(HEADS)]
+        slopes(0)
+        slopes(1)
+        for i in range(0, len(units), 2):
+            if i + 2 < len(units):
+                slopes(i + 2)
+                slopes(i + 3)
+            spread(i)
+            spread(i + 1)
+            b = units[i][0]
+            if units[i + 1][3] < HEADS - 1:
+                continue
             if b + 1 < count and (False or not last):
                 input_back(b + 1)
                 if not last and True:
@@ -660,7 +667,7 @@
     keep_extra = pltpu.make_async_copy(grads.at[1 - part, half_rows], extra_hbm.at[part], in_sem.at[2])
     keep_grad.start()
     keep_extra.start()
-    for action in "DUSDUSQDUSQDUSQDU":
+    for action in "SDUSQDUSQDUSQDU":
         perform(action)
 
     state_copy().wait()
@@ -789,6 +796,8 @@
             V(SPAN + BLOCK, BLOCK, dtype=f32),
             V(SPAN + BLOCK, BLOCK, dtype=f32),
             V(SPAN + BLOCK, BLOCK, dtype=f32),
+            V(SPAN + BLOCK, BLOCK),
+            V(SPAN + BLOCK, BLOCK),
             V(SPAN + BLOCK, BLOCK),
             V(SPAN + BLOCK, BLOCK),
             V(length, width, dtype=f32),

time: 75.6 us -> 75.5 us (level)
  no operation moved by 1% of the time
where the time goes in v6:
time: 75.5 us; the launch traced here: 75.3 us
  Pallas kernels  74.5 us (99%)
  between operations  0.84 us (1%)
    pallas_call x1, Pallas kernels, whole_block(): pl.pallas_call(partial(compute_kernel, far_count), name='block_both_ways'...  69.5 us
    pallas_call x1, Pallas kernels, whole_block(): pl.pallas_call(finish_kernel, name='widen', in_specs=[hbm] * 7, out_specs...  5.05 us

profile of v6, /device:TPU:0, one launch (start us, length us, event | category | flops | bytes accessed | tf_op | source)
XLA Modules:
  0.0 75.3 jit_solution(764502785770647497)
XLA Ops:
  0.7 69.5 %block_both_ways.1 = (bf16[2,1024,256]{2,1,0:T(8,128)(2,1)}, bf16[2,1024,256]{2,1,0:T(8,128)(2,1)}, bf16[2,512,256]{2,1,0:T(8,128)(2,1)}, bf16[2048,128]{1,0:T(8...) custom-call(bf16[2,1024,256]{2,1,0:T(8,128)(2,1)} %start_hbm.1, ...), custom_call_target="tpu_custom_call" | custom-call | tf_op jit(solution)/shard_map/block_both_ways/pallas_call | solution.py:776
  70.1 5.0 %widen.1 = (bf16[1,2,1024,256]{3,2,1,0:T(8,128)(2,1)}, f32[1,2,1024,256]{3,2,1,0:T(8,128)}, f32[2,512,256]{2,1,0:T(8,128)}, f32[256]{0:T(256)}, f32[256]{0:T(256...) custom-call(bf16[2,1024,256]{2,1,0:T(8,128)(2,1)} %get-tuple-element, ...), custom_call_target="tpu_custom_call" | custom-call | tf_op jit(solution)/shard_map/widen/pallas_call | solution.py:856
